TPU v7x, 32 devices: a whole 2x2x4 slice. The times are simulated.
32 devices in a mesh: dp: 4 (over y, x), mp: 8 (over z, core).
Axes of the slice: x: 2, y: 2, z: 4, core: 2. Of those that a mesh axis runs over, the one named last changes fastest.
Arguments:
- tokens: bfloat16 [2, 4096, 2048], P(None, ('dp', 'mp')), may hold values from -6 to 6
- doc_ids: int32 [2, 4096], P(None, 'dp'), may hold values from 0 to 15, never falling along the last dimension, each value on 1 to 1024 neighbouring positions
- cotangent: bfloat16 [2, 4096, 2048], P(None, ('dp', 'mp')), may hold values from -6 to 6
- norm1_gain: bfloat16 [2048], P(('dp', 'mp')), may hold values from 0.25 to 1.75
- norm1_bias: bfloat16 [2048], P(('dp', 'mp')), may hold values from -3 to 3
- query_weight: bfloat16 [2048, 2048], P('dp', 'mp'), may hold values from -0.125 to 0.125
- query_bias: bfloat16 [16, 128], P('mp', 'dp'), may hold values from -3 to 3
- kv_weight: bfloat16 [2048, 256], P(('dp', 'mp')), may hold values from -0.125 to 0.125
- value_bias: bfloat16 [128], P(('dp', 'mp')), may hold values from -3 to 3
- out_weight: bfloat16 [2048, 2048], P('mp', 'dp'), may hold values from -1 to 1
- out_bias: bfloat16 [2048], P(('dp', 'mp')), may hold values from -3 to 3
- norm2_gain: bfloat16 [2048], P(('dp', 'mp')), may hold values from 0.25 to 1.75
- norm2_bias: bfloat16 [2048], P(('dp', 'mp')), may hold values from -3 to 3
- up_weight: bfloat16 [2048, 8192], P('dp', 'mp'), may hold values from -0.125 to 0.125
- up_bias: bfloat16 [64, 128], P('mp', 'dp'), may hold values from -3 to 3
- down_weight: bfloat16 [8192, 2048], P('mp', 'dp'), may hold values from -0.5 to 0.5
- down_bias: bfloat16 [2048], P(('dp', 'mp')), may hold values from -3 to 3
Outputs:
- output: bfloat16 [2, 4096, 2048], P(None, ('dp', 'mp'))
- input_grad: bfloat16 [2, 4096, 2048], P(None, ('dp', 'mp'))
- norm1_gain_grad: float32 [2048], P(('dp', 'mp'))
- norm1_bias_grad: float32 [2048], P(('dp', 'mp'))
- query_weight_grad: float32 [2048, 2048], P('dp', 'mp')
- query_bias_grad: float32 [16, 128], P('mp', 'dp')
- kv_weight_grad: float32 [2048, 256], P(('dp', 'mp'))
- value_bias_grad: float32 [128], P(('dp', 'mp'))
- out_weight_grad: float32 [2048, 2048], P('mp', 'dp')
- out_bias_grad: float32 [2048], P(('dp', 'mp'))
- norm2_gain_grad: float32 [2048], P(('dp', 'mp'))
- norm2_bias_grad: float32 [2048], P(('dp', 'mp'))
- up_weight_grad: float32 [2048, 8192], P('dp', 'mp')
- up_bias_grad: float32 [64, 128], P('mp', 'dp')
- down_weight_grad: float32 [8192, 2048], P('mp', 'dp')
- down_bias_grad: float32 [2048], P(('dp', 'mp'))
Inputs may be any that keep to these rules, and one draw needn't show every extreme that they name: `doc_ids`: along the 4096 tokens of a micro-batch the ids never fall, so each document's tokens are consecutive; a document holds 1 to 1024 tokens.
All inputs are finite; a program needn't handle non-finite values.
Results may differ from a plain program's by a relative error of at most 0.023.
Values may be sent and summed in bfloat16 or wider, within the bound.
No kernel may reach another device: no remote copies, remote signals or barrier semaphores. Data moves between devices by JAX's collectives and lax.ppermute only.
A program may use at most 96 MiB of HBM per device.

v0:
```python
import jax
import jax.numpy as jnp
from jax import lax
from jax.sharding import PartitionSpec as P

HD = 128


EPSILON = 1e-05


def layer_norm(tok_rows, norm_gain, norm_shift):
    row_mean = jnp.mean(tok_rows, axis=-1, keepdims=True)
    centred = tok_rows - row_mean
    row_var = jnp.mean(centred * centred, axis=-1, keepdims=True)
    return centred * lax.rsqrt(row_var + EPSILON) * norm_gain + norm_shift


def norm_back(tok_rows, norm_gain, norm_shift, grad_rows):
    norm_out, pullback = jax.vjp(layer_norm, tok_rows, norm_gain, norm_shift)
    return pullback(grad_rows)


def gelu_tanh(values):
    return jax.nn.gelu(values, approximate=True)


def contract(left, right, left_dim, right_dim):
    return lax.dot_general(
        left, right, (((left_dim,), (right_dim,)), ((), ())), preferred_element_type=jnp.float32
    )


def block_scores(query_heads, key_rows, doc_row, block_start, block_len):
    query_block = lax.dynamic_slice_in_dim(query_heads, block_start, block_len, 0)
    query_docs = lax.dynamic_slice_in_dim(doc_row, block_start, block_len, 0)
    query_pos = block_start + jnp.arange(block_len, dtype=jnp.int32)
    key_pos = jnp.arange(doc_row.shape[0], dtype=jnp.int32)
    allowed = (query_docs[:, None] == doc_row[None, :]) & (key_pos[None, :] <= query_pos[:, None])
    scores = jnp.einsum(
        "qhd,kd->hqk", query_block, key_rows, preferred_element_type=jnp.float32
    ) * HD ** (-0.5)
    return (query_block, jnp.where(allowed[None], scores, -1e30))


def add_parts(running, addend):
    if running is None:
        return addend
    return jax.tree.map(jnp.add, running, addend)


def reduce_layer(grad_parts):
    return (
        lax.psum_scatter(
            grad_parts[0].astype(jnp.bfloat16), "dp", scatter_dimension=0, tiled=True
        ).astype(jnp.float32),
        lax.psum_scatter(
            grad_parts[1].astype(jnp.bfloat16), "dp", scatter_dimension=1, tiled=True
        ).astype(jnp.float32),
        lax.psum_scatter(
            grad_parts[2].astype(jnp.bfloat16), "dp", scatter_dimension=1, tiled=True
        ).astype(jnp.float32),
        lax.psum_scatter(
            grad_parts[3].astype(jnp.bfloat16), "dp", scatter_dimension=0, tiled=True
        ).astype(jnp.float32),
        lax.psum_scatter(
            grad_parts[4].astype(jnp.bfloat16), "dp", scatter_dimension=1, tiled=True
        ).astype(jnp.float32),
        lax.psum_scatter(
            grad_parts[5].astype(jnp.bfloat16), "dp", scatter_dimension=1, tiled=True
        ).astype(jnp.float32),
    )


def reduce_shared(grad_parts):
    return (
        lax.psum_scatter(grad_parts[0], ("dp", "mp"), scatter_dimension=0, tiled=True),
        lax.psum_scatter(grad_parts[1], ("dp", "mp"), scatter_dimension=0, tiled=True),
        lax.psum_scatter(grad_parts[2], ("dp", "mp"), scatter_dimension=0, tiled=True),
        lax.psum_scatter(grad_parts[3], ("dp", "mp"), scatter_dimension=0, tiled=True),
        lax.psum_scatter(grad_parts[4], ("dp", "mp"), scatter_dimension=0, tiled=True),
        lax.psum_scatter(grad_parts[5], ("dp", "mp"), scatter_dimension=0, tiled=True),
        lax.psum_scatter(grad_parts[6], ("dp", "mp"), scatter_dimension=0, tiled=True),
        lax.psum_scatter(grad_parts[7], ("dp", "mp"), scatter_dimension=0, tiled=True),
    )


def on_device(
    tokens,
    doc_ids,
    cotangent,
    norm1_gain,
    norm1_bias,
    query_weight,
    query_bias,
    kv_weight,
    value_bias,
    out_weight,
    out_bias,
    norm2_gain,
    norm2_bias,
    up_weight,
    up_bias,
    down_weight,
    down_bias,
):
    window = doc_ids.shape[1]
    block_len = min(512, window)
    starts = jnp.arange(window // block_len, dtype=jnp.int32) * block_len
    score_scale = HD ** (-0.5)
    shared = (
        lax.all_gather(kv_weight, ("dp", "mp"), axis=0, tiled=True),
        lax.all_gather(norm1_gain, ("dp", "mp"), axis=0, tiled=True),
        lax.all_gather(norm1_bias, ("dp", "mp"), axis=0, tiled=True),
        lax.all_gather(out_bias, ("dp", "mp"), axis=0, tiled=True),
        lax.all_gather(norm2_gain, ("dp", "mp"), axis=0, tiled=True),
        lax.all_gather(norm2_bias, ("dp", "mp"), axis=0, tiled=True),
        lax.all_gather(down_bias, ("dp", "mp"), axis=0, tiled=True),
        lax.all_gather(value_bias, ("dp", "mp"), axis=0, tiled=True),
    )
    kv_full = shared[0]
    gain_one, shift_one, out_shift, gain_two, shift_two, down_shift, value_shift = (
        member.astype(jnp.float32) for member in shared[1:]
    )
    kv_shift = jnp.concatenate([jnp.zeros((HD,), jnp.float32), value_shift])
    outputs = []
    input_grads = []
    layer_total = None
    shared_total = None
    for micro_index in range(tokens.shape[0]):
        gathered = (
            lax.all_gather(query_weight, "dp", axis=0, tiled=True),
            lax.all_gather(query_bias, "dp", axis=1, tiled=True),
            lax.all_gather(out_weight, "dp", axis=1, tiled=True),
            lax.all_gather(up_weight, "dp", axis=0, tiled=True),
            lax.all_gather(up_bias, "dp", axis=1, tiled=True),
            lax.all_gather(down_weight, "dp", axis=1, tiled=True),
        )
        query_full, query_table, out_full, up_full, up_table, down_full = gathered
        query_shift = query_table.astype(jnp.float32).reshape(-1)
        up_shift = up_table.astype(jnp.float32).reshape(-1)
        local_heads = query_full.shape[1] // HD
        tok_rows = tokens[micro_index].astype(jnp.float32)
        doc_row = doc_ids[micro_index]
        normed = layer_norm(tok_rows, gain_one, shift_one).astype(jnp.bfloat16)
        normed_all = lax.all_gather(normed, "mp", axis=0, tiled=True)
        kv_rows = (
            jnp.dot(normed_all, kv_full, preferred_element_type=jnp.float32) + kv_shift
        ).astype(jnp.bfloat16)
        key_rows = kv_rows[:, :HD]
        value_rows = kv_rows[:, HD:]
        query_heads = (
            (jnp.dot(normed_all, query_full, preferred_element_type=jnp.float32) + query_shift)
            .astype(jnp.bfloat16)
            .reshape(window, local_heads, HD)
        )

        def attend(block_start):
            query_block, scores = block_scores(
                query_heads, key_rows, doc_row, block_start, block_len
            )
            row_max = jnp.max(scores, axis=-1, keepdims=True)
            weights = jnp.exp(scores - row_max)
            row_total = jnp.sum(weights, axis=-1, keepdims=True)
            probs_low = (weights / row_total).astype(jnp.bfloat16)
            context_block = jnp.einsum(
                "hqk,kd->qhd", probs_low, value_rows, preferred_element_type=jnp.float32
            )
            return (context_block, row_max + jnp.log(row_total))

        context_blocks, log_totals = lax.map(attend, starts)
        context = context_blocks.reshape(window, local_heads * HD).astype(jnp.bfloat16)
        middle = (
            tok_rows
            + lax.psum_scatter(
                jnp.dot(context, out_full, preferred_element_type=jnp.float32).astype(jnp.bfloat16),
                "mp",
                scatter_dimension=0,
                tiled=True,
            ).astype(jnp.float32)
            + out_shift
        )
        normed_two = layer_norm(middle, gain_two, shift_two).astype(jnp.bfloat16)
        normed_two_all = lax.all_gather(normed_two, "mp", axis=0, tiled=True)
        pre_act = jnp.dot(normed_two_all, up_full, preferred_element_type=jnp.float32) + up_shift
        hidden_full, gelu_pull = jax.vjp(gelu_tanh, pre_act)
        hidden = hidden_full.astype(jnp.bfloat16)
        result = (
            middle
            + lax.psum_scatter(
                jnp.dot(hidden, down_full, preferred_element_type=jnp.float32).astype(jnp.bfloat16),
                "mp",
                scatter_dimension=0,
                tiled=True,
            ).astype(jnp.float32)
            + down_shift
        )
        outputs.append(result.astype(jnp.bfloat16))
        grad_out = cotangent[micro_index]
        grad_all = lax.all_gather(grad_out, "mp", axis=0, tiled=True)
        hidden_grad = contract(grad_all, down_full, 1, 1)
        pre_grad = gelu_pull(hidden_grad)[0].astype(jnp.bfloat16)
        down_grad = contract(hidden, grad_all, 0, 0)
        up_grad = contract(normed_two_all, pre_grad, 0, 0)
        up_bias_grad = jnp.sum(pre_grad, axis=0, dtype=jnp.float32).reshape(up_table.shape)
        normed_two_grad = lax.psum_scatter(
            contract(pre_grad, up_full, 1, 1).astype(jnp.bfloat16),
            "mp",
            scatter_dimension=0,
            tiled=True,
        ).astype(jnp.float32)
        middle_part, gain_two_grad, shift_two_grad = norm_back(
            middle, gain_two, shift_two, normed_two_grad
        )
        middle_grad = grad_out.astype(jnp.float32) + middle_part
        down_bias_grad = jnp.sum(grad_out, axis=0, dtype=jnp.float32)
        middle_low = middle_grad.astype(jnp.bfloat16)
        middle_all = lax.all_gather(middle_low, "mp", axis=0, tiled=True)
        out_bias_grad = jnp.sum(middle_low, axis=0, dtype=jnp.float32)
        context_grad = contract(middle_all, out_full, 1, 1).astype(jnp.bfloat16)
        out_grad = contract(context, middle_all, 0, 0)
        context_heads = context_grad.reshape(window, local_heads, HD)

        def attend_back(grad_carry, inputs):
            key_grad, value_grad = grad_carry
            block_start, log_total = inputs
            query_block, scores = block_scores(
                query_heads, key_rows, doc_row, block_start, block_len
            )
            probs_full = jnp.exp(scores - log_total)
            probs_low = probs_full.astype(jnp.bfloat16)
            grad_block = lax.dynamic_slice_in_dim(context_heads, block_start, block_len, 0)
            probs_grad = jnp.einsum(
                "qhd,kd->hqk", grad_block, value_rows, preferred_element_type=jnp.float32
            )
            row_dot = jnp.sum(probs_full * probs_grad, axis=-1, keepdims=True)
            score_grad = (probs_full * (probs_grad - row_dot)).astype(jnp.bfloat16)
            query_part = (
                jnp.einsum("hqk,kd->qhd", score_grad, key_rows, preferred_element_type=jnp.float32)
                * score_scale
            ).astype(jnp.bfloat16)
            key_part = (
                jnp.einsum(
                    "hqk,qhd->kd", score_grad, query_block, preferred_element_type=jnp.float32
                )
                * score_scale
            )
            value_part = jnp.einsum(
                "hqk,qhd->kd", probs_low, grad_block, preferred_element_type=jnp.float32
            )
            return ((key_grad + key_part, value_grad + value_part), query_part)

        zero_rows = jnp.zeros((window, HD), jnp.float32)
        (key_grad, value_grad), query_blocks = lax.scan(
            attend_back, (zero_rows, zero_rows), (starts, log_totals)
        )
        query_grad = query_blocks.reshape(window, local_heads * HD)
        kv_grad_rows = lax.psum_scatter(
            jnp.concatenate([key_grad, value_grad], axis=1).astype(jnp.bfloat16),
            "mp",
            scatter_dimension=0,
            tiled=True,
        )
        query_weight_grad = contract(normed_all, query_grad, 0, 0)
        query_bias_grad = jnp.sum(query_grad, axis=0, dtype=jnp.float32).reshape(query_table.shape)
        normed_grad = lax.psum_scatter(
            contract(query_grad, query_full, 1, 1).astype(jnp.bfloat16),
            "mp",
            scatter_dimension=0,
            tiled=True,
        ).astype(jnp.float32) + contract(kv_grad_rows, kv_full, 1, 1)
        kv_weight_grad = contract(normed, kv_grad_rows, 0, 0)
        value_bias_grad = jnp.sum(kv_grad_rows[:, HD:], axis=0, dtype=jnp.float32)
        rows_part, gain_one_grad, shift_one_grad = norm_back(
            tok_rows, gain_one, shift_one, normed_grad
        )
        input_grads.append((middle_grad + rows_part).astype(jnp.bfloat16))
        layer_parts = (
            query_weight_grad,
            query_bias_grad,
            out_grad,
            up_grad,
            up_bias_grad,
            down_grad,
        )
        shared_parts = (
            kv_weight_grad,
            gain_one_grad,
            shift_one_grad,
            out_bias_grad,
            gain_two_grad,
            shift_two_grad,
            down_bias_grad,
            value_bias_grad,
        )
        layer_total = add_parts(layer_total, reduce_layer(layer_parts))
        shared_total = add_parts(shared_total, reduce_shared(shared_parts))
    return (
        jnp.stack(outputs),
        jnp.stack(input_grads),
        shared_total[1],
        shared_total[2],
        layer_total[0],
        layer_total[1],
        shared_total[0],
        shared_total[7],
        layer_total[2],
        shared_total[3],
        shared_total[4],
        shared_total[5],
        layer_total[3],
        layer_total[4],
        layer_total[5],
        shared_total[6],
    )


def solution(mesh):
    in_specs = (
        P(None, ("dp", "mp"), None),
        P(None, "dp"),
        P(None, ("dp", "mp"), None),
        P(("dp", "mp")),
        P(("dp", "mp")),
        P("dp", "mp"),
        P("mp", "dp"),
        P(("dp", "mp"), None),
        P(("dp", "mp")),
        P("mp", "dp"),
        P(("dp", "mp")),
        P(("dp", "mp")),
        P(("dp", "mp")),
        P("dp", "mp"),
        P("mp", "dp"),
        P("mp", "dp"),
        P(("dp", "mp")),
    )
    out_specs = (
        P(None, ("dp", "mp"), None),
        P(None, ("dp", "mp"), None),
        P(("dp", "mp")),
        P(("dp", "mp")),
        P("dp", "mp"),
        P("mp", "dp"),
        P(("dp", "mp"), None),
        P(("dp", "mp")),
        P("mp", "dp"),
        P(("dp", "mp")),
        P(("dp", "mp")),
        P(("dp", "mp")),
        P("dp", "mp"),
        P("mp", "dp"),
        P("mp", "dp"),
        P(("dp", "mp")),
    )
    return jax.shard_map(
        on_device, mesh=mesh, in_specs=in_specs, out_specs=out_specs, check_vma=False
    )
```

profile of v0, /device:TPU:0, one launch (start us, length us, event | category | flops | bytes accessed | tf_op | source)
XLA Modules:
  0.0 1715.6 jit_solution(10387766006919816769)
XLA Ops:
  13.9 42.7 %all-reduce.16 = (bf16[2048]{0:T(1024)(128)(2,1)S(1)}, bf16[2048]{0:T(1024)(128)(2,1)S(1)}, bf16[128]{0:T(256)(128)(2,1)S(1)}, bf16[2048]{0:T(1024)(128)(2,1)S(1...) all-reduce(bf16[2048]{0:T(1024)(128)(2,1)S(1)} %dynamic-update-slic, ...), channel_id=1, replica_groups=mesh['dp'=4,'mp'=8] {'dp','mp'}, use_global_device_ids=true, to_apply=%add.2 | all-reduce | flops 12416 | bytes 49664
  73.8 42.0 %all-gather.18.cloned.1.call-done = bf16[1024,2048]{1,0:T(8,128)(2,1)} async-done(((bf16[128,2048]{1,0:T(8,128)(2,1)}), bf16[1024,2048]{1,0:T(8,128)(2,1)}) %all-gather.18.cloned.1.call-update) | async-done | bytes 4194320 | tf_op jit(solution)/shard_map/all_gather | solution.py:146
  176.0 50.1 %reduce-scatter.32.cloned.1.call-done = bf16[128,2048]{1,0:T(8,128)(2,1)} async-done(((bf16[1024,2048]{1,0:T(8,128)(2,1)}), bf16[128,2048]{1,0:T(8,128)(2,1)}) %reduce-scatter.32.cloned.1.call-update) | async-done | bytes 524304 | tf_op jit(solution)/shard_map/reduce_scatter | solution.py:175
  229.0 45.2 %all-gather.32.cloned.1.call-done = bf16[1024,2048]{1,0:T(8,128)(2,1)} async-done(((bf16[128,2048]{1,0:T(8,128)(2,1)}), bf16[1024,2048]{1,0:T(8,128)(2,1)}) %all-gather.32.cloned.1.call-update) | async-done | bytes 4194320 | tf_op jit(solution)/shard_map/all_gather | solution.py:146
  306.3 48.0 %reduce-scatter.36.cloned.1.call-done = bf16[128,2048]{1,0:T(8,128)(2,1)} async-done(((bf16[1024,2048]{1,0:T(8,128)(2,1)}), bf16[128,2048]{1,0:T(8,128)(2,1)}) %reduce-scatter.36.cloned.1.call-update) | async-done | bytes 524304 | tf_op jit(solution)/shard_map/reduce_scatter | solution.py:175
  371.4 35.7 %all-gather.28.cloned.1.call-done = bf16[2048,1024]{1,0:T(8,128)(2,1)} async-done(((bf16[512,1024]{1,0:T(8,128)(2,1)}), bf16[2048,1024]{1,0:T(8,128)(2,1)}) %all-gather.28.cloned.1.call-update) | async-done | bytes 4194320 | tf_op jit(solution)/shard_map/all_gather | solution.py:135
  407.1 49.4 %all-gather.34.cloned.1.call-done = bf16[1024,2048]{1,0:T(8,128)(2,1)} async-done(((bf16[128,2048]{1,0:T(8,128)(2,1)}), bf16[1024,2048]{1,0:T(8,128)(2,1)}) %all-gather.34.cloned.1.call-update) | async-done | bytes 4194320 | tf_op jit(solution)/shard_map/all_gather | solution.py:184
  466.4 43.1 %all-gather.30.cloned.1.call-done = bf16[1024,2048]{1,0:T(8,128)(2,1)} async-done(((bf16[1024,512]{1,0:T(8,128)(2,1)}), bf16[1024,2048]{1,0:T(8,128)(2,1)}) %all-gather.30.cloned.1.call-update) | async-done | bytes 4194320 | tf_op jit(solution)/shard_map/all_gather | solution.py:137
  509.5 49.4 %all-gather.42.cloned.1.call-done = bf16[1,1024,2048]{2,1,0:T(8,128)(2,1)} async-done(((bf16[1,128,2048]{2,1,0:T(8,128)(2,1)}), bf16[1,1024,2048]{2,1,0:T(8,128)(2,1)}) %all-gather.42.cloned.1.call-update) | async-done | bytes 4194320 | tf_op jit(solution)/shard_map/all_gather | solution.py:200
  616.7 38.2 %all-gather.40.cloned.1.call-done = bf16[1,1024,2048]{2,1,0:T(8,128)(2,1)} async-done(((bf16[1,128,2048]{2,1,0:T(8,128)(2,1)}), bf16[1,1024,2048]{2,1,0:T(8,128)(2,1)}) %all-gather.40.cloned.1.call-update) | async-done | bytes 4194320 | tf_op jit(solution)/shard_map/all_gather | solution.py:200
  705.8 50.3 %reduce-scatter.40.cloned.1.call-done = bf16[128,2048]{1,0:T(8,128)(2,1)} async-done(((bf16[1024,2048]{1,0:T(8,128)(2,1)}), bf16[128,2048]{1,0:T(8,128)(2,1)}) %reduce-scatter.40.cloned.1.call-update) | async-done | bytes 524304 | tf_op jit(solution)/shard_map/reduce_scatter | solution.py:206
  759.1 47.3 %reduce-scatter.34.cloned.1.call-done = bf16[128,2048]{1,0:T(8,128)(2,1)} async-done(((bf16[1024,2048]{1,0:T(8,128)(2,1)}), bf16[128,2048]{1,0:T(8,128)(2,1)}) %reduce-scatter.34.cloned.1.call-update) | async-done | bytes 524304 | tf_op jit(solution)/shard_map/reduce_scatter | solution.py:190
  809.3 47.4 %reduce-scatter.38.cloned.1.call-done = bf16[128,2048]{1,0:T(8,128)(2,1)} async-done(((bf16[1024,2048]{1,0:T(8,128)(2,1)}), bf16[128,2048]{1,0:T(8,128)(2,1)}) %reduce-scatter.38.cloned.1.call-update) | async-done | bytes 524304 | tf_op jit(solution)/shard_map/reduce_scatter | solution.py:190
  911.2 36.3 %while.56 = (s32[]{:T(128)}, f32[1024,128]{1,0:T(8,128)}, f32[1024,128]{1,0:T(8,128)}, bf16[2,512,2,128]{3,1,2,0:T(8,128)(2,1)}, s32[2]{0:T(128)S(1)}, /*index=5...) while((s32[]{:T(128)}, f32[1024,128]{1,0:T(8,128)}, ...), condition=%wide.region_25.26_spmd.clone, body=%wide.region_23.25_spmd.clone.sunk | while | flops 1360395776 | bytes 80783808 | solution.py:254
  959.0 34.7 %while.57 = (s32[]{:T(128)}, f32[1024,128]{1,0:T(8,128)S(1)}, f32[1024,128]{1,0:T(8,128)}, bf16[2,512,2,128]{3,1,2,0:T(8,128)(2,1)}, s32[2]{0:T(128)S(1)}, /*ind...) while((s32[]{:T(128)}, f32[1024,128]{1,0:T(8,128)S(1)}, ...), condition=%wide.region_35.36_spmd.clone, body=%wide.region_33.35_spmd.clone.sunk | while | flops 1360395776 | bytes 80783808 | solution.py:254
  1062.0 56.0 %reduce-scatter.62.cloned.1.call-done = bf16[512,1024]{1,0:T(8,128)(2,1)} async-done(((bf16[2048,1024]{1,0:T(8,128)(2,1)}), bf16[512,1024]{1,0:T(8,128)(2,1)}) %reduce-scatter.62.cloned.1.call-update) | async-done | bytes 1048592 | tf_op jit(solution)/shard_map/reduce_scatter | solution.py:63
  1188.5 48.4 %reduce-scatter.64.cloned.1.call-done = bf16[1024,512]{1,0:T(8,128)(2,1)} async-done(((bf16[1024,2048]{1,0:T(8,128)(2,1)}), bf16[1024,512]{1,0:T(8,128)(2,1)}) %reduce-scatter.64.cloned.1.call-update) | async-done | bytes 1048592 | tf_op jit(solution)/shard_map/reduce_scatter | solution.py:69
  1236.9 55.7 %reduce-scatter.66.cloned.1.call-done = bf16[1024,512]{1,0:T(8,128)(2,1)} async-done(((bf16[1024,2048]{1,0:T(8,128)(2,1)}), bf16[1024,512]{1,0:T(8,128)(2,1)}) %reduce-scatter.66.cloned.1.call-update) | async-done | bytes 1048592 | tf_op jit(solution)/shard_map/reduce_scatter | solution.py:69
  1376.0 30.9 %reduce-scatter.56.cloned.1.call-done = bf16[256,512]{1,0:T(8,128)(2,1)} async-done(((bf16[256,2048]{1,0:T(8,128)(2,1)}), bf16[256,512]{1,0:T(8,128)(2,1)}) %reduce-scatter.56.cloned.1.call-update) | async-done | bytes 262160 | tf_op jit(solution)/shard_map/reduce_scatter | solution.py:60
  1437.6 30.7 %reduce-scatter.54.cloned.1.call-done = bf16[512,256]{1,0:T(8,128)(2,1)} async-done(((bf16[2048,256]{1,0:T(8,128)(2,1)}), bf16[512,256]{1,0:T(8,128)(2,1)}) %reduce-scatter.54.cloned.1.call-update) | async-done | bytes 262160 | tf_op jit(solution)/shard_map/reduce_scatter | solution.py:54
  1470.2 50.5 %reduce-scatter.48.cloned.1.call-done = bf16[128,2048]{1,0:T(8,128)(2,1)} async-done(((bf16[1024,2048]{1,0:T(8,128)(2,1)}), bf16[128,2048]{1,0:T(8,128)(2,1)}) %reduce-scatter.48.cloned.1.call-update) | async-done | bytes 524304 | tf_op jit(solution)/shard_map/reduce_scatter | solution.py:266
  1523.1 48.0 %reduce-scatter.42.cloned.1.call-done = bf16[128,2048]{1,0:T(8,128)(2,1)} async-done(((bf16[1024,2048]{1,0:T(8,128)(2,1)}), bf16[128,2048]{1,0:T(8,128)(2,1)}) %reduce-scatter.42.cloned.1.call-update) | async-done | bytes 524304 | tf_op jit(solution)/shard_map/reduce_scatter | solution.py:266
  1574.8 39.1 %all-reduce.15 = (f32[2048]{0:T(1024)S(1)}, f32[2048]{0:T(1024)S(1)}, f32[128]{0:T(128)S(1)}, f32[2048]{0:T(1024)S(1)}, f32[2048]{0:T(1024)S(1)}, /*index=5*/f32[2048]{0:T(1024)S(1)}, f32[2048]{0:T(1024)S(1)}) all-reduce(f32[2048]{0:T(1024)S(1)} %add.487, f32[2048]{0:T(1024)S(1)} %add.488, ...), channel_id=22, replica_groups=mesh['dp'=4,'mp'=8] {'dp','mp'}, use_global_device_ids=true, to_apply=%region_41.42.clone | all-reduce | flops 12416 | bytes 99328
  1621.9 86.9 %reduce-scatter.68.cloned.1.call-done = f32[64,256]{1,0:T(8,128)} async-done(((f32[2048,256]{1,0:T(8,128)}), f32[64,256]{1,0:T(8,128)}) %reduce-scatter.68.cloned.1.call-update) | async-done | bytes 65552 | tf_op jit(solution)/shard_map/reduce_scatter | solution.py:77
  (518 shorter events, 682.0 us)
Async XLA Ops:
  360.6 198.3 %all-gather.42.cloned.1.call-start = ((), (), s32[]{:S(2)}) async-start(), calls=%async_computation.53 | async-start | bytes 4718592 | tf_op jit(solution)/shard_map/all_gather | solution.py:200
  361.7 245.1 %all-gather.26.cloned.1.call-start = ((), (), s32[]{:S(2)}) async-start(), calls=%async_computation.28 | async-start | bytes 4718592 | tf_op jit(solution)/shard_map/all_gather | solution.py:184
  362.3 292.6 %all-gather.40.cloned.1.call-start = ((), (), s32[]{:S(2)}) async-start(), calls=%async_computation.52 | async-start | bytes 4718592 | tf_op jit(solution)/shard_map/all_gather | solution.py:200
  363.0 342.7 %reduce-scatter.46.cloned.1.call-start = ((), (), s32[]{:S(2)}) async-start(), calls=%async_computation.40 | async-start | bytes 4718592 | tf_op jit(solution)/shard_map/reduce_scatter | solution.py:206
  578.1 178.0 %reduce-scatter.40.cloned.1.call-start = ((), (), s32[]{:S(2)}) async-start(), calls=%async_computation.36 | async-start | bytes 4718592 | tf_op jit(solution)/shard_map/reduce_scatter | solution.py:206
  684.8 171.9 %reduce-scatter.38.cloned.1.call-start = ((), (), s32[]{:S(2)}) async-start(), calls=%async_computation.35 | async-start | bytes 4718592 | tf_op jit(solution)/shard_map/reduce_scatter | solution.py:190
  695.4 211.4 %all-gather.36.cloned.1.call-start = ((), (), s32[]{:S(2)}) async-start(), calls=%async_computation.37 | async-start | bytes 4718592 | tf_op jit(solution)/shard_map/all_gather | solution.py:218
  862.1 186.4 %reduce-scatter.74.cloned.1.call-start = ((), (), s32[]{:S(2)}) async-start(), calls=%async_computation.57 | async-start | bytes 40960
  862.9 186.4 %reduce-scatter.76.cloned.1.call-start = ((), (), s32[]{:S(2)}) async-start(), calls=%async_computation.58 | async-start | bytes 40960
  863.7 198.3 %reduce-scatter.60.cloned.1.call-start = ((), (), s32[]{:S(2)}) async-start(), calls=%async_computation.48 | async-start | bytes 5242880 | tf_op jit(solution)/shard_map/reduce_scatter | solution.py:63
  873.6 244.4 %reduce-scatter.62.cloned.1.call-start = ((), (), s32[]{:S(2)}) async-start(), calls=%async_computation.49 | async-start | bytes 5242880 | tf_op jit(solution)/shard_map/reduce_scatter | solution.py:63
  883.6 267.6 %reduce-scatter.44.cloned.1.call-start = ((), (), s32[]{:S(2)}) async-start(), calls=%async_computation.39 | async-start | bytes 589824 | tf_op jit(solution)/shard_map/reduce_scatter | solution.py:258
  950.6 232.7 %reduce-scatter.50.cloned.1.call-start = ((), (), s32[]{:S(2)}) async-start(), calls=%async_computation.43 | async-start | bytes 589824 | tf_op jit(solution)/shard_map/reduce_scatter | solution.py:258
  995.6 241.2 %reduce-scatter.64.cloned.1.call-start = ((), (), s32[]{:S(2)}) async-start(), calls=%async_computation.50 | async-start | bytes 5242880 | tf_op jit(solution)/shard_map/reduce_scatter | solution.py:69
  1006.5 286.1 %reduce-scatter.66.cloned.1.call-start = ((), (), s32[]{:S(2)}) async-start(), calls=%async_computation.51 | async-start | bytes 5242880 | tf_op jit(solution)/shard_map/reduce_scatter | solution.py:69
  1017.3 301.6 %reduce-scatter.70.cloned.1.call-start = ((), (), s32[]{:S(2)}) async-start(), calls=%async_computation.55 | async-start | bytes 40960
  1019.3 326.2 %reduce-scatter.72.cloned.1.call-start = ((), (), s32[]{:S(2)}) async-start(), calls=%async_computation.56 | async-start | bytes 40960
  1020.3 355.7 %reduce-scatter.58.cloned.1.call-start = ((), (), s32[]{:S(2)}) async-start(), calls=%async_computation.47 | async-start | bytes 1310720 | tf_op jit(solution)/shard_map/reduce_scatter | solution.py:60
  1024.8 382.1 %reduce-scatter.56.cloned.1.call-start = ((), (), s32[]{:S(2)}) async-start(), calls=%async_computation.46 | async-start | bytes 1310720 | tf_op jit(solution)/shard_map/reduce_scatter | solution.py:60
  1029.6 408.0 %reduce-scatter.52.cloned.1.call-start = ((), (), s32[]{:S(2)}) async-start(), calls=%async_computation.44 | async-start | bytes 1310720 | tf_op jit(solution)/shard_map/reduce_scatter | solution.py:54
  1034.9 433.3 %reduce-scatter.54.cloned.1.call-start = ((), (), s32[]{:S(2)}) async-start(), calls=%async_computation.45 | async-start | bytes 1310720 | tf_op jit(solution)/shard_map/reduce_scatter | solution.py:54
  1040.2 480.4 %reduce-scatter.48.cloned.1.call-start = ((), (), s32[]{:S(2)}) async-start(), calls=%async_computation.42 | async-start | bytes 4718592 | tf_op jit(solution)/shard_map/reduce_scatter | solution.py:266
  1043.7 527.4 %reduce-scatter.42.cloned.1.call-start = ((), (), s32[]{:S(2)}) async-start(), calls=%async_computation.38 | async-start | bytes 4718592 | tf_op jit(solution)/shard_map/reduce_scatter | solution.py:266
  1047.1 661.7 %reduce-scatter.68.cloned.1.call-start = ((), (), s32[]{:S(2)}) async-start(), calls=%async_computation.54 | async-start | bytes 2162688 | tf_op jit(solution)/shard_map/reduce_scatter | solution.py:77
  (114 other events, 5680.1 us)
Sparse Core Ops, SparseCore 0:
  11.0 56.4 all-gather.21
  69.7 46.1 all-gather.17
  176.0 50.0 reduce-scatter.31
  228.9 45.2 all-gather.31
  305.6 48.7 reduce-scatter.35
  356.2 50.8 all-gather.27
  409.3 47.1 all-gather.33
  458.2 51.2 all-gather.29
  511.7 47.1 all-gather.41
  560.9 45.8 all-gather.25
  609.0 45.8 all-gather.39
  657.0 48.7 reduce-scatter.45
  707.9 48.1 reduce-scatter.39
  758.2 48.1 reduce-scatter.33
  808.5 48.1 reduce-scatter.37
  861.5 45.2 all-gather.35
  908.4 45.8 all-gather.37
  1009.3 52.6 reduce-scatter.59
  1065.3 52.6 reduce-scatter.61
  1186.0 50.7 reduce-scatter.63
  1240.0 52.6 reduce-scatter.65
  1470.6 50.0 reduce-scatter.47
  1522.9 48.1 reduce-scatter.41
  1573.8 134.9 reduce-scatter.67
  (12 shorter events, 315.1 us)
where the time goes:
time: 1720 us
  waiting for transfers between devices  1230 us (72%)
  matrix products  237 us (14%)
  blocking collectives  99.4 us (6%)
  other arithmetic  68.1 us (4%)
  local copies, waits for them, and re-layouts  44.4 us (3%)
    dot_general x20, matrix products, contract(): lax.dot_general(left, right, (((left_dim,), (right_dim,)), ((), ())), pre...  117 us
    reduce_scatter x2, waiting for transfers between devices, reduce_layer(): lax.psum_scatter(grad_parts[5].astype(jnp.bfloat16), 'dp', scatter_dimens...  104 us
    reduce_scatter x2, waiting for transfers between devices, on_device(): lax.psum_scatter(contract(query_grad, query_full, 1, 1).astype(jnp.bfloat...  98.4 us
    reduce_scatter x2, waiting for transfers between devices, on_device(): lax.psum_scatter(jnp.dot(context, out_full, preferred_element_type=jnp.fl...  98.1 us
    reduce_scatter x2, waiting for transfers between devices, on_device(): lax.psum_scatter(jnp.dot(hidden, down_full, preferred_element_type=jnp.fl...  94.7 us
    all_gather x2, waiting for transfers between devices, on_device(): grad_all = lax.all_gather(grad_out, 'mp', axis=0, tiled=True)  87.5 us
    all_gather x2, waiting for transfers between devices, on_device(): normed_all = lax.all_gather(normed, 'mp', axis=0, tiled=True)  87.2 us
    reduce_scatter x1, waiting for transfers between devices, reduce_shared(): lax.psum_scatter(grad_parts[0], ('dp', 'mp'), scatter_dimension=0, tiled=...  86.9 us
  transfers between devices with their start and end apart: 36, of which 33 were waited for; matrix products, arithmetic and copies ran while one was open for 17% of the time, Pallas kernels for 0%

commit v1 on v0

v1 whole, which is shorter than its diff:
```python
import jax
import jax.numpy as jnp
from jax import lax
from jax.experimental import pallas as pl
from jax.experimental.pallas import tpu as pltpu
from jax.sharding import PartitionSpec as P

HD = 128
EPSILON = 1e-05
LOW = jnp.bfloat16
WIDE = jnp.float32


def norm_stats(rows):
    mean = jnp.mean(rows, axis=-1, keepdims=True)
    centred = rows - mean
    var = jnp.mean(centred * centred, axis=-1, keepdims=True)
    scale = lax.rsqrt(var + EPSILON)
    return centred * scale, scale


def norm_forward(rows, gain, shift):
    xhat, scale = norm_stats(rows)
    return xhat * gain + shift


def norm_backward(rows, gain, grad):
    xhat, scale = norm_stats(rows)
    scaled = grad * gain
    inner = (
        scaled
        - jnp.mean(scaled, axis=-1, keepdims=True)
        - xhat * jnp.mean(scaled * xhat, axis=-1, keepdims=True)
    )
    return scale * inner, jnp.sum(grad * xhat, axis=0), jnp.sum(grad, axis=0)


def gelu_pair(values):
    inner = 0.7978845608028654 * (values + 0.044715 * values * values * values)
    bent = jnp.tanh(inner)
    half = 0.5 * (1.0 + bent)
    slope = half + 0.5 * values * (1.0 - bent * bent) * 0.7978845608028654 * (
        1.0 + 3.0 * 0.044715 * values * values
    )
    return values * half, slope


def contract(left, right, left_dim, right_dim):
    return lax.dot_general(
        left, right, (((left_dim,), (right_dim,)), ((), ())), preferred_element_type=WIDE
    )


def swap_core(block):
    count = lax.axis_size("mp")
    return lax.ppermute(block, "mp", [(i, i ^ 1) for i in range(count)])


def shift_line(block, hops):
    count = lax.axis_size("mp")
    return lax.ppermute(block, "mp", [(i, (i + 2 * hops) % count) for i in range(count)])


def swap_dp(block, bit):
    count = lax.axis_size("dp")
    return lax.ppermute(block, "dp", [(i, i ^ bit) for i in range(count)])


def swap_mp(block, bit):
    count = lax.axis_size("mp")
    return lax.ppermute(block, "mp", [(i, i ^ bit) for i in range(count)])


def fence(*values):
    return lax.optimization_barrier(values)


def line_pairs(moves):
    return [(2 * source + side, 2 * target + side) for source, target in moves for side in (0, 1)]


def line_order():
    count = lax.axis_size("mp") // 2
    line = lax.axis_index("mp") // 2
    if count == 4:
        low_side = line < 2
        return [line, line ^ 1, jnp.where(low_side, 2, 1), jnp.where(low_side, 3, 0)]
    return [(line + count - step) % count for step in range(count)]


def line_near(block):
    count = lax.axis_size("mp") // 2
    if count == 4:
        return jnp.concatenate([block, swap_mp(block, 2)], axis=0)
    return jnp.concatenate([block] + [shift_line(block, i) for i in range(1, count // 2)], axis=0)


def line_across(block, near):
    count = lax.axis_size("mp") // 2
    if count == 4:
        return lax.ppermute(near, "mp", line_pairs([(1, 2), (2, 1)]))
    return jnp.concatenate([shift_line(block, i) for i in range(count // 2, count)], axis=0)


def line_out(across):
    if lax.axis_size("mp") // 2 == 4:
        line = lax.axis_index("mp") // 2
        outward = lax.ppermute(across, "mp", line_pairs([(1, 0), (2, 3)]))
        return jnp.where((line == 1) | (line == 2), across, outward)
    return across


def middle_swap(block):
    return lax.ppermute(block, "mp", line_pairs([(1, 2), (2, 1)]))


def move_out(block):
    return lax.ppermute(block, "mp", line_pairs([(1, 0), (2, 3)]))


def move_in(block):
    return lax.ppermute(block, "mp", line_pairs([(0, 1), (3, 2)]))


def plus(left, right):
    return (left.astype(WIDE) + right.astype(WIDE)).astype(LOW)


def four_places():
    return lax.axis_size("mp") // 2 == 4


def gather_1(own):
    if four_places():
        return swap_mp(own, 2), middle_swap(own)
    count = lax.axis_size("mp") // 2
    near = [own] + [shift_line(own, i) for i in range(1, count // 2)]
    far = [shift_line(own, i) for i in range(count // 2, count)]
    return jnp.concatenate(near, axis=0), jnp.concatenate(far, axis=0)


def gather_near(own, first):
    return jnp.concatenate([own, first[0]], axis=0) if four_places() else first[0]


def gather_2(first):
    return (middle_swap(first[0]), move_out(first[1])) if four_places() else first


def gather_3(first, second):
    if not four_places():
        return first[1]
    line = lax.axis_index("mp") // 2
    inner = (line == 1) | (line == 2)
    last = move_out(second[0])
    return jnp.concatenate(
        [jnp.where(inner, first[1], second[1]), jnp.where(inner, second[0], last)], axis=0
    )


def reduce_1(far):
    return move_in(far[far.shape[0] // 2 :]) if four_places() else far


def reduce_2(far, got):
    if not four_places():
        return got, got
    size = far.shape[0] // 2
    return middle_swap(plus(far[size:], got)), move_in(far[:size])


def reduce_3(near, far, got):
    if four_places():
        size = near.shape[0] // 2
        return (
            swap_mp(plus(near[size:], got[0]), 2),
            middle_swap(plus(far[:size], got[1])),
        )
    count = lax.axis_size("mp") // 2
    size = near.shape[0] * 2 // count
    blocks = [half[i * size : (i + 1) * size] for half in (near, far) for i in range(count // 2)]
    return [shift_line(blocks[hops], -hops) for hops in range(1, count)]


def reduce_end(near, got):
    total = near[: got[0].shape[0]].astype(WIDE)
    for part in got:
        total = total + part.astype(WIDE)
    return total


def sum_inward(far):
    return move_in(far) if four_places() else far


def add_inward(far, got):
    return plus(far, got) if four_places() else far


def sum_across(near, passed):
    if not four_places():
        return near, passed
    size = near.shape[0] // 2
    across = middle_swap(passed)
    return near[:size].astype(WIDE) + across[:size].astype(WIDE), plus(near[size:], across[size:])


def sum_last(first, second):
    if four_places():
        return first + swap_mp(second, 2).astype(WIDE)
    return reduce_end(first, reduce_3(first, second, None))


def dp_first(block):
    count = lax.axis_size("dp")
    if count == 4:
        return [block, swap_dp(block, 1), swap_dp(block, 2)]
    blocks = [block]
    bit = 1
    while bit < count:
        size = block.shape[0]
        got = swap_dp(jnp.concatenate(blocks, axis=0), bit)
        blocks = blocks + [got[i * size : (i + 1) * size] for i in range(bit)]
        bit = bit * 2
    return blocks


def dp_second(blocks):
    if lax.axis_size("dp") == 4:
        half = blocks[0].shape[0] // 2
        head, tail = swap_dp(blocks[1][:half], 2), swap_dp(blocks[2][half:], 1)
        return list(blocks) + [jnp.concatenate([head, tail], axis=0)]
    return list(blocks)


def dp_sum_first(blocks):
    if len(blocks) == 4:
        half = blocks[0].shape[0] // 2
        head = swap_dp(blocks[3][:half], 2).astype(WIDE)
        tail = swap_dp(blocks[3][half:], 1).astype(WIDE)
        one = jnp.concatenate(
            [(blocks[1][:half].astype(WIDE) + head).astype(LOW), blocks[1][half:]], axis=0
        )
        two = jnp.concatenate(
            [blocks[2][:half], (blocks[2][half:].astype(WIDE) + tail).astype(LOW)], axis=0
        )
        return [blocks[0], one, two]
    bit = len(blocks) // 2
    size = blocks[0].shape[0]
    while bit >= 1:
        got = swap_dp(jnp.concatenate(blocks[bit:], axis=0), bit).astype(WIDE)
        blocks = [
            (blocks[i].astype(WIDE) + got[i * size : (i + 1) * size]).astype(LOW)
            for i in range(bit)
        ]
        bit = bit // 2
    return blocks


def dp_sum_second(blocks):
    total = blocks[0].astype(WIDE)
    for bit, block in enumerate(blocks[1:]):
        total = total + swap_dp(block, bit + 1).astype(WIDE)
    return total


def pack_reduce(parts):
    place = lax.axis_index("mp")
    bit = parts.shape[0] // 2
    while bit >= 1:
        parts = parts[:bit] + swap_dp(parts[bit:], bit)
        bit = bit // 2
    parts = parts[0]
    bit = parts.shape[0] // 2
    while bit >= 1:
        upper = (place & bit) != 0
        low_half, high_half = parts[:bit], parts[bit:]
        sent = swap_mp(jnp.where(upper, low_half, high_half), bit)
        parts = jnp.where(upper, high_half, low_half) + sent
        bit = bit // 2
    return parts[0]


def relative(array, axis):
    count = lax.axis_size("dp")
    place = lax.axis_index("dp")
    size = array.shape[axis] // count
    return jnp.concatenate(
        [
            lax.dynamic_slice_in_dim(array, (place ^ step) * size, size, axis)
            for step in range(count)
        ],
        axis=axis,
    )


def held(array):
    zeros = (0,) * array.ndim
    return pl.BlockSpec(array.shape, lambda *_: zeros, pipeline_mode=pl.Buffered(1))


def shaped(shape, dtype=LOW):
    return jax.ShapeDtypeStruct(shape, dtype)


def attend_kernel(n, cells, *refs):
    (own, other), refs = refs[:2], refs[2:]
    weights, refs = refs[:n], refs[n:]
    shift, keyval, query_doc, query_pos, key_doc, key_pos, query, context, probs, bias = refs
    head = pl.program_id(0)
    heads, rows, _ = query.shape
    places, size = cells

    @pl.when(head == 0)
    def _():
        allowed = (query_doc[...] == key_doc[...]) & (key_pos[...] <= query_pos[...])
        bias[...] = jnp.where(allowed, 0.0, -1e30)
        chip = jnp.concatenate([own[...], other[...]], axis=0)
        cols = weights[0].shape[1]
        for place in range(places):
            total = None
            for block in range(n):
                term = contract(
                    chip[:, block * size : (block + 1) * size],
                    weights[block][place * size : (place + 1) * size, :],
                    1,
                    0,
                )
                total = term if total is None else total + term
            total = (total + shift[:, place * cols : (place + 1) * cols]).astype(LOW)
            for i in range(cols // HD):
                query[place * (cols // HD) + i] = total[:, i * HD : (i + 1) * HD]

    scores = contract(query[head], keyval[:, :HD], 1, 1) * HD ** (-0.5) + bias[...]
    weight = jnp.exp(scores - jnp.max(scores, axis=-1, keepdims=True))
    share = 1.0 / jnp.sum(weight, axis=-1, keepdims=True)
    low = (weight * share).astype(LOW)
    probs[0] = low
    context[...] = contract(low, keyval[:, HD:], 1, 0).astype(LOW)


def attend(own, other, weights, shift, keyval, query_doc, query_pos, key_doc, key_pos):
    rows, width = own.shape
    rows = 2 * rows
    keys = keyval.shape[0]
    n = len(weights)
    size = width // n
    places = weights[0].shape[0] // size
    heads = places * weights[0].shape[1] // HD
    operands = [own, other, *weights, shift[None], keyval]
    operands += [query_doc[:, None], query_pos[:, None], key_doc[None], key_pos[None]]
    return pl.pallas_call(
        lambda *refs: attend_kernel(n, (places, size), *refs),
        grid=(heads,),
        in_specs=[held(o) for o in operands],
        out_specs=[
            pl.BlockSpec((heads, rows, HD), lambda h: (0, 0, 0)),
            pl.BlockSpec((rows, HD), lambda h: (0, h)),
            pl.BlockSpec((1, rows, keys), lambda h: (h, 0, 0)),
        ],
        out_shape=[
            shaped((heads, rows, HD)),
            shaped((rows, heads * HD)),
            shaped((heads, rows, keys)),
        ],
        scratch_shapes=[pltpu.VMEM((rows, keys), WIDE)],
        compiler_params=pltpu.CompilerParams(vmem_limit_bytes=18 * 2**20),
        cost_estimate=pl.CostEstimate(
            flops=4 * rows * keys * heads * HD + 2 * rows * width * heads * HD,
            bytes_accessed=2 * heads * rows * keys + 2 * width * heads * HD,
            transcendentals=heads * rows * keys,
        ),
    )(*operands)


def project_kernel(n, *refs):
    context, weights, (own, other) = refs[0], refs[1 : 1 + n], refs[1 + n :]
    rows = own.shape[0]
    size = weights[0].shape[1]
    for block in range(n):
        cols = slice(block * size, (block + 1) * size)
        got = contract(context[...], weights[block][...], 1, 0)
        own[:, cols] = got[:rows]
        other[:, cols] = got[rows:].astype(LOW)


def project(context, weights):
    n = len(weights)
    rows, depth = context.shape
    width = n * weights[0].shape[1]
    return pl.pallas_call(
        lambda *refs: project_kernel(n, *refs),
        out_shape=[shaped((rows // 2, width), WIDE), shaped((rows // 2, width))],
        compiler_params=pltpu.CompilerParams(vmem_limit_bytes=20 * 2**20),
        cost_estimate=pl.CostEstimate(
            flops=2 * rows * depth * width, bytes_accessed=2 * depth * width, transcendentals=0
        ),
    )(context, *weights)


def attend_back_kernel(n, heads, cells, *refs):
    (own, other), refs = refs[:2], refs[2:]
    out_weights, refs = refs[:n], refs[n:]
    query_weights, refs = refs[:n], refs[n:]
    query, keyval, probs, refs = refs[0], refs[1], refs[2], refs[3:]
    query_grad, keyval_grad, back_own, back_other, context_grad, all_grad, total = refs
    head = pl.program_id(0)
    scale = HD ** (-0.5)
    places, size = cells

    @pl.when(head == 0)
    def _():
        total[...] = jnp.zeros_like(total)
        chip = jnp.concatenate([own[...], other[...]], axis=0)
        got = None
        for block in range(n):
            term = contract(chip[:, block * size : (block + 1) * size], out_weights[block][...], 1, 1)
            got = term if got is None else got + term
        got = got.astype(LOW)
        for i in range(heads):
            context_grad[i] = got[:, i * HD : (i + 1) * HD]

    low = probs[0]
    wide = low.astype(WIDE)
    given = contract(context_grad[head], keyval[:, HD:], 1, 1)
    middle = jnp.sum(wide * given, axis=-1, keepdims=True)
    score_grad = (wide * (given - middle)).astype(LOW)
    moved = (contract(score_grad, keyval[:, :HD], 1, 0) * scale).astype(LOW)
    query_grad[...] = moved
    all_grad[head] = moved
    total[:, :HD] += contract(score_grad, query[head], 0, 0)
    total[:, HD:] += contract(low, context_grad[head], 0, 0)

    @pl.when(head == heads - 1)
    def _():
        keyval_grad[:, :HD] = (total[:, :HD] * scale).astype(LOW)
        keyval_grad[:, HD:] = total[:, HD:].astype(LOW)
        cols = query_weights[0].shape[1]
        each = cols // HD
        parts = [
            jnp.concatenate([all_grad[place * each + i] for i in range(each)], axis=1)
            for place in range(places)
        ]
        rows = back_own.shape[0]
        for block in range(n):
            got = None
            for place in range(places):
                term = contract(
                    parts[place], query_weights[block][place * size : (place + 1) * size, :], 1, 1
                )
                got = term if got is None else got + term
            back_own[:, block * size : (block + 1) * size] = got[:rows]
            back_other[:, block * size : (block + 1) * size] = got[rows:].astype(LOW)


def attend_back(own, other, out_weights, query_weights, query, keyval, probs):
    rows, width = own.shape
    heads, both, _ = query.shape
    keys = keyval.shape[0]
    n = len(out_weights)
    size = width // n
    places = query_weights[0].shape[0] // size
    first = [own, other, *out_weights, *query_weights, query, keyval]
    return pl.pallas_call(
        lambda *refs: attend_back_kernel(n, heads, (places, size), *refs),
        grid=(heads,),
        in_specs=[held(o) for o in first] + [pl.BlockSpec((1, both, keys), lambda h: (h, 0, 0))],
        out_specs=[
            pl.BlockSpec((both, HD), lambda h: (0, h)),
            pl.BlockSpec((keys, 2 * HD), lambda h: (0, 0)),
            pl.BlockSpec((rows, width), lambda h: (0, 0)),
            pl.BlockSpec((rows, width), lambda h: (0, 0)),
        ],
        out_shape=[
            shaped((both, heads * HD)),
            shaped((keys, 2 * HD)),
            shaped((rows, width), WIDE),
            shaped((rows, width)),
        ],
        scratch_shapes=[
            pltpu.VMEM((heads, both, HD), LOW),
            pltpu.VMEM((heads, both, HD), LOW),
            pltpu.VMEM((keys, 2 * HD), WIDE),
        ],
        compiler_params=pltpu.CompilerParams(vmem_limit_bytes=48 * 2**20),
        cost_estimate=pl.CostEstimate(
            flops=8 * both * keys * heads * HD + 4 * both * width * heads * HD,
            bytes_accessed=2 * heads * both * keys + 4 * width * heads * HD,
            transcendentals=0,
        ),
    )(*first, probs)


def mlp_kernel(n, *refs):
    rows_in, refs = refs[:2], refs[2:]
    grads_in, refs = refs[:2], refs[2:]
    ups, refs = refs[:n], refs[n:]
    downs, refs = refs[:n], refs[n:]
    shift, hidden, pre_grad, back, out, other = refs
    size = ups[0].shape[0]
    count = rows_in[0].shape[0]
    spans = [slice(i * size, (i + 1) * size) for i in range(n)]
    for side in (1, 0):
        pre = given = None
        for block, span in enumerate(spans):
            term = contract(rows_in[side][:, span], ups[block][...], 1, 0)
            pre = term if pre is None else pre + term
        for block, span in enumerate(spans):
            term = contract(grads_in[side][:, span], downs[block][...], 1, 1)
            given = term if given is None else given + term
        value, slope = gelu_pair(pre + shift[...])
        value = value.astype(LOW)
        grad = (given * slope).astype(LOW)
        hidden[side * count : (side + 1) * count] = value
        pre_grad[side * count : (side + 1) * count] = grad
        for block, span in enumerate(spans):
            got = contract(grad, ups[block][...], 1, 1).astype(LOW)
            if side == 0:
                back[:, span] = got
            else:
                other[:count, span] = got
        for block, span in enumerate(spans):
            got = contract(value, downs[block][...], 1, 0).astype(LOW)
            if side == 0:
                out[:, span] = got
            else:
                other[count:, span] = got


def mlp(rows_in, grads_in, ups, downs, shift):
    n = len(ups)
    count, width = rows_in[0].shape
    units = ups[0].shape[1]
    return pl.pallas_call(
        lambda *refs: mlp_kernel(n, *refs),
        out_shape=[shaped((2 * count, units))] * 2
        + [shaped((count, width))] * 2
        + [shaped((2 * count, width))],
        compiler_params=pltpu.CompilerParams(vmem_limit_bytes=34 * 2**20),
        cost_estimate=pl.CostEstimate(
            flops=16 * count * units * width,
            bytes_accessed=4 * units * width + 16 * count * width,
            transcendentals=2 * count * units,
        ),
    )(*rows_in, *grads_in, *ups, *downs, shift[None])


def up_grad_kernel(n, *refs):
    lefts, rights, result = refs[:n], refs[n : -1], refs[-1]
    per = n // len(rights)
    total = None
    for i, right in enumerate(rights):
        count = right.shape[0] // per
        for j in range(per):
            term = contract(lefts[i * per + j][...], right[j * count : (j + 1) * count], 0, 0)
            total = term if total is None else total + term
    result[0] = total.astype(LOW)


def up_grad_of(lefts, rights, blocks):
    count, width = lefts[0].shape
    units = rights[0].shape[1]
    size = width // blocks
    n = len(lefts)
    return pl.pallas_call(
        lambda *refs: up_grad_kernel(n, *refs),
        grid=(blocks,),
        in_specs=[pl.BlockSpec((count, size), lambda b: (0, b))] * n + [held(r) for r in rights],
        out_specs=pl.BlockSpec((1, size, units), lambda b: (b, 0, 0)),
        out_shape=shaped((blocks, size, units)),
        compiler_params=pltpu.CompilerParams(vmem_limit_bytes=44 * 2**20),
        cost_estimate=pl.CostEstimate(
            flops=2 * n * count * width * units,
            bytes_accessed=2 * (n * count * (width + units) + width * units),
            transcendentals=0,
        ),
    )(*lefts, *rights)


def down_grad_kernel(n, *refs):
    lefts, rights, result = refs[: -n - 1], refs[-n - 1 : -1], refs[-1]
    per = n // len(lefts)
    blocks, _, size = result.shape
    for block in range(blocks):
        total = None
        for i, left in enumerate(lefts):
            count = left.shape[0] // per
            for j in range(per):
                term = contract(
                    left[j * count : (j + 1) * count],
                    rights[i * per + j][:, block * size : (block + 1) * size],
                    0,
                    0,
                )
                total = term if total is None else total + term
        result[block] = total.astype(LOW)


def down_grad_of(lefts, rights, blocks):
    count, width = rights[0].shape
    rows, units = lefts[0].shape
    n = len(rights)
    tile = min(256, units)
    return pl.pallas_call(
        lambda *refs: down_grad_kernel(n, *refs),
        grid=(units // tile,),
        in_specs=[pl.BlockSpec((rows, tile), lambda u: (0, u))] * len(lefts)
        + [held(r) for r in rights],
        out_specs=pl.BlockSpec((blocks, tile, width // blocks), lambda u: (0, u, 0)),
        out_shape=shaped((blocks, units, width // blocks)),
        compiler_params=pltpu.CompilerParams(vmem_limit_bytes=44 * 2**20),
        cost_estimate=pl.CostEstimate(
            flops=2 * n * count * width * units,
            bytes_accessed=2 * (n * count * (width + units) + width * units),
            transcendentals=0,
        ),
    )(*lefts, *rights)


def on_device(
    tokens,
    doc_ids,
    cotangent,
    norm1_gain,
    norm1_bias,
    query_weight,
    query_bias,
    kv_weight,
    value_bias,
    out_weight,
    out_bias,
    norm2_gain,
    norm2_bias,
    up_weight,
    up_bias,
    down_weight,
    down_bias,
):
    n_dp, n_mp = lax.axis_size("dp"), lax.axis_size("mp")
    n_line = n_mp // 2
    dp, mp = lax.axis_index("dp"), lax.axis_index("mp")
    line, core = mp // 2, mp % 2
    micro, rows, width = tokens.shape
    window = doc_ids.shape[1]
    part = norm1_gain.shape[0]
    kv_part = kv_weight.shape[0]
    heads_part = query_bias.shape[0]
    units_part = up_bias.shape[0]
    slim = query_bias.shape[1]

    flat = micro * rows
    lanes = 2 * HD
    order = line_order()
    tok_low = relative(tokens, 2)
    cot_low = relative(cotangent, 2)
    vectors = [norm1_gain, norm1_bias, out_bias, norm2_gain, norm2_bias, down_bias]
    vectors += [value_bias, query_bias.reshape(-1), up_bias.reshape(-1)]
    table = jnp.stack([jnp.pad(v, (0, lanes - v.shape[0])) for v in vectors])
    table = jnp.pad(table, ((0, 16 - len(vectors)), (0, 0)))
    pack = lax.all_gather(
        jnp.concatenate([kv_weight, table], axis=0), ("dp", "mp"), axis=0, tiled=True
    )

    def back_sum(got, swapped):
        return plus(got[2], swapped[: got[2].shape[0]])

    def out_sum_of(got, swapped):
        return plus(got[3], swapped[got[3].shape[0] :])

    query_near = line_near(query_weight)
    out_near = line_near(out_weight)
    up_first = dp_first(up_weight)
    query_near, out_near, cot_low, tok_low = fence(query_near, out_near, cot_low, tok_low)
    query_across = line_across(query_weight, query_near)
    cot_near = [line_near(cot_low[0])]
    query_across, out_near, cot_near, up_first = fence(query_across, out_near, cot_near, up_first)
    query_far = line_out(query_across)
    out_across = line_across(out_weight, out_near)
    up_blocks = dp_second(up_first)
    query_far, out_across, cot_near, up_blocks = fence(query_far, out_across, cot_near, up_blocks)
    query_first = dp_first(jnp.concatenate([query_near, query_far], axis=0))
    out_far = line_out(out_across)
    cot_across = [line_across(cot_low[0], cot_near[0])]
    cot_near.append(line_near(cot_low[1]))
    (pack,) = fence(pack)
    pack = pack.reshape(n_dp, n_mp, kv_part + 16, lanes)
    kv_full = relative(pack[:, :, :kv_part], 0).reshape(width, lanes)
    fixed = pack[:, :, kv_part:].astype(WIDE)
    small = relative(fixed, 0)
    gain_one, shift_one, out_shift, gain_two, shift_two, down_shift = (
        small[:, :, i, :part].reshape(width) for i in range(6)
    )
    tok_rows = [tok_low[m].astype(WIDE) for m in range(micro)]
    normed = jnp.stack([norm_forward(r, gain_one, shift_one).astype(LOW) for r in tok_rows])
    normed_other = swap_core(normed)
    query_first, out_far, normed_other, kv_full, cot_across, fixed, cot_near = fence(
        query_first, out_far, normed_other, kv_full, cot_across, fixed, cot_near
    )
    query_blocks = dp_second(query_first)
    value_shift = fixed[:, :, 6, : value_bias.shape[0]].reshape(HD)
    kv_shift = jnp.concatenate([jnp.zeros((HD,), WIDE), value_shift])
    kv_own = (contract(normed.reshape(flat, width), kv_full, 1, 0) + kv_shift).astype(LOW)
    kv_near = line_near(kv_own)
    kv_near, out_line, fixed, cot_low = fence(
        kv_near, jnp.concatenate([out_near, out_far], axis=0), fixed, cot_low
    )
    out_first = dp_first(out_line)
    kv_across = line_across(kv_own, kv_near)
    query_table = fixed[:, :, 7, : heads_part * slim].reshape(
        n_dp, n_line, 2, heads_part, slim
    )
    query_table = lax.dynamic_index_in_dim(query_table, core, 2, keepdims=False)
    query_table = query_table.transpose(1, 2, 0, 3).reshape(n_line, heads_part * HD)
    query_shift = jnp.concatenate(
        [lax.dynamic_index_in_dim(query_table, spot, 0, keepdims=False) for spot in order]
    )
    query_blocks, kv_across, query_shift = fence(query_blocks, kv_across, query_shift)
    kv_line = jnp.concatenate([kv_near, line_out(kv_across)], axis=0)
    kv_line = kv_line.reshape(n_line, flat, lanes)
    kv_stack = jnp.stack([kv_line, swap_core(kv_line)], axis=1)
    kv_stack = kv_stack.reshape(n_line, 2, micro, rows, lanes)
    keyval = [kv_stack[:, :, m].reshape(window, lanes) for m in range(micro)]
    keyval, cot_across = fence(keyval, cot_across)
    cot_far = [line_out(cot_across[0])]
    cot_across.append(line_across(cot_low[1], cot_near[1]))
    cot_own = [swap_core(cot_near[0])]
    key_starts = [(spot * 2 + side) * rows for spot in order for side in (core, 1 - core)]
    key_pos = jnp.concatenate([s + jnp.arange(rows, dtype=jnp.int32) for s in key_starts])
    query_pos = key_pos[: 2 * rows]
    context, probs, query = [], [], []
    for m in range(micro):
        key_doc = jnp.concatenate(
            [lax.dynamic_slice_in_dim(doc_ids[m], s, rows, 0) for s in key_starts]
        )
        got = attend(
            normed[m],
            normed_other[m],
            query_blocks,
            query_shift,
            keyval[m],
            key_doc[: 2 * rows],
            query_pos,
            key_doc,
            key_pos,
        )
        query.append(got[0])
        context.append(got[1])
        probs.append(got[2])
    out_first, context, cot_own, cot_far, cot_across = fence(
        out_first, context, cot_own, cot_far, cot_across
    )
    out_blocks = dp_second(out_first)
    cot_far.append(line_out(cot_across[1]))
    out_blocks, context, down_own, fixed = fence(out_blocks, context, down_weight, fixed)
    down_first = dp_first(down_own)
    middle, normed_two = [], []
    for m in range(micro):
        mine, theirs = project(context[m], out_blocks)
        middle.append(tok_rows[m] + out_shift + mine + swap_core(theirs).astype(WIDE))
        normed_two.append(norm_forward(middle[m], gain_two, shift_two).astype(LOW))
    normed_two, fixed = fence(normed_two, fixed)
    first = [gather_1(normed_two[0])]
    up_table = lax.dynamic_index_in_dim(
        fixed[:, :, 8, : units_part * slim], mp, 1, keepdims=False
    ).reshape(n_dp, units_part, slim)
    up_shift = up_table.transpose(1, 0, 2).reshape(units_part * HD)
    first, normed_two, down_first, up_shift, cot_far = fence(
        first, normed_two, down_first, up_shift, cot_far
    )
    near_rows = [gather_near(normed_two[0], first[0])]
    near_other = [swap_core(near_rows[0])]
    second = [gather_2(first[0])]
    down_blocks = dp_second(down_first)
    near_rows, near_other, second, down_blocks, cot_far, cot_near = fence(
        near_rows, near_other, second, down_blocks, cot_far, cot_near
    )

    def feed(m, half):
        rows_in = (near_rows[m], near_other[m]) if half == 0 else (far_rows[m], far_other[m])
        grads_in = (cot_near[m], cot_own[m]) if half == 0 else (cot_far[m], cot_other[m])
        return mlp(rows_in, grads_in, up_blocks, down_blocks, up_shift)

    far_rows = [gather_3(first[0], second[0])]
    cot_other = [swap_core(cot_far[0])]
    near_got = [feed(0, 0)]
    far_rows, near_got, normed_two, cot_other = fence(far_rows, near_got, normed_two, cot_other)
    first.append(gather_1(normed_two[1]))
    far_other = [swap_core(far_rows[0])]
    near_swap = [swap_core(near_got[0][4])]
    cot_own.append(swap_core(cot_near[1]))
    far_got = [feed(0, 1)]
    first, far_got, near_swap, near_got, cot_own = fence(
        first, far_got, near_swap, near_got, cot_own
    )
    second.append(gather_2(first[1]))
    far_swap = [swap_core(far_got[0][4])]
    near_rows.append(gather_near(normed_two[1], first[1]))
    near_other.append(swap_core(near_rows[1]))
    near_back = [back_sum(near_got[0], near_swap[0])]
    near_out = [out_sum_of(near_got[0], near_swap[0])]
    second, near_rows, near_other, far_swap, near_back, near_out, cot_far = fence(
        second, near_rows, near_other, far_swap, near_back, near_out, cot_far
    )
    far_back = [back_sum(far_got[0], far_swap[0])]
    far_rows.append(gather_3(first[1], second[1]))
    got_1 = [reduce_1(far_back[0])]
    cot_other.append(swap_core(cot_far[1]))
    near_got.append(feed(1, 0))
    far_rows, got_1, near_got, far_back, cot_other, far_swap = fence(
        far_rows, got_1, near_got, far_back, cot_other, far_swap
    )
    got_2 = [reduce_2(far_back[0], got_1[0])]
    far_out = [out_sum_of(far_got[0], far_swap[0])]
    far_other.append(swap_core(far_rows[1]))
    near_swap.append(swap_core(near_got[1][4]))
    far_got.append(feed(1, 1))
    got_2, near_swap, far_got, near_got, far_out = fence(
        got_2, near_swap, far_got, near_got, far_out
    )
    got_3 = [reduce_3(near_back[0], far_back[0], got_2[0])]
    far_swap.append(swap_core(far_got[1][4]))
    near_back.append(back_sum(near_got[1], near_swap[1]))
    pre_grad = [g[1] for m in range(micro) for g in (near_got[m], far_got[m])]
    row_pieces = [
        p
        for m in range(micro)
        for p in (near_rows[m], near_other[m], far_rows[m], far_other[m])
    ]
    up_grad = up_grad_of(row_pieces, pre_grad, n_dp)
    got_3, far_swap, up_grad, near_back, near_swap = fence(
        got_3, far_swap, up_grad, near_back, near_swap
    )
    far_back.append(back_sum(far_got[1], far_swap[1]))
    got_1.append(reduce_1(far_back[1]))
    up_sum = dp_sum_first([up_grad[i] for i in range(n_dp)])
    got_3, near_swap, far_swap, up_sum = fence(got_3, near_swap, far_swap, up_sum)
    near_out.append(out_sum_of(near_got[1], near_swap[1]))
    back = [reduce_end(near_back[0], got_3[0])]
    middle_grad, middle_low, middle_other = [], [], []
    norm_two_grads = []
    query_grad, keyval_grad, backs = [], [], []

    def middle_step(m):
        moved, gain_part, shift_part = norm_backward(middle[m], gain_two, back[m])
        middle_grad.append(cot_low[m].astype(WIDE) + moved)
        middle_low.append(middle_grad[m].astype(LOW))
        norm_two_grads.append((gain_part, shift_part))
        middle_other.append(swap_core(middle_low[m]))

    def attend_step(m):
        got = attend_back(
            middle_low[m], middle_other[m], out_blocks, query_blocks, query[m], keyval[m], probs[m]
        )
        query_grad.append(got[0])
        keyval_grad.append(got[1].reshape(n_line, 2, rows, lanes))
        backs.append(list(got[2:]))

    middle_step(0)
    got_1, middle_low, middle_other, far_back, far_swap, near_out, up_sum = fence(
        got_1, middle_low, middle_other, far_back, far_swap, near_out, up_sum
    )
    got_2.append(reduce_2(far_back[1], got_1[1]))
    up_weight_grad = dp_sum_second(up_sum)
    attend_step(0)
    far_out.append(out_sum_of(far_got[1], far_swap[1]))
    hidden = [g[0] for m in range(micro) for g in (near_got[m], far_got[m])]
    got_2, query_grad, hidden, far_out = fence(got_2, query_grad, hidden, far_out)
    got_3.append(reduce_3(near_back[1], far_back[1], got_2[1]))
    backs[0][1] = swap_core(backs[0][1])
    cot_pieces = [
        p for m in range(micro) for p in (cot_near[m], cot_own[m], cot_far[m], cot_other[m])
    ]
    down_grad = down_grad_of(hidden, cot_pieces, n_dp)
    got_3, down_grad, backs, up_weight_grad, far_out = fence(
        got_3, down_grad, backs, up_weight_grad, far_out
    )
    down_sum = dp_sum_first([down_grad[i] for i in range(n_dp)])
    out_inward = [sum_inward(far_out[0])]
    back.append(reduce_end(near_back[1], got_3[1]))
    middle_step(1)
    middle_low, middle_other = fence(middle_low, middle_other)

    def over_micro(left, right):
        total = contract(left[0], right[0], 0, 0)
        for m in range(1, len(left)):
            total = total + contract(left[m], right[m], 0, 0)
        return total.astype(LOW)

    out_grad = over_micro(
        context, [jnp.concatenate([middle_low[m], middle_other[m]], axis=0) for m in range(micro)]
    )
    out_grad, down_sum, far_out = fence(out_grad, down_sum, far_out)
    middle_low[1] = fence(middle_low[1], out_grad)[0]
    out_size = out_weight.shape[1]
    out_sum = dp_sum_first([out_grad[:, i * out_size : (i + 1) * out_size] for i in range(n_dp)])
    out_inward.append(sum_inward(far_out[1]))
    attend_step(1)
    query_grad, keyval_grad, out_sum, backs = fence(query_grad, keyval_grad, out_sum, backs)
    out_sum = dp_sum_second(out_sum).astype(LOW)
    query_sum = over_micro(
        [jnp.concatenate([normed[m], normed_other[m]], axis=0) for m in range(micro)], query_grad
    )
    kv_parts = jnp.stack(keyval_grad, axis=2)
    kv_swapped = swap_core(kv_parts[:, 1])
    backs[1][1] = swap_core(backs[1][1])
    query_size, query_cols = query_weight.shape
    query_sums = [
        jnp.concatenate(
            [
                query_sum[
                    i * query_size : (i + 1) * query_size, j * query_cols : (j + 1) * query_cols
                ]
                for j in range(n_line)
            ],
            axis=0,
        )
        for i in range(n_dp)
    ]
    kv_swapped, query_sums, backs, out_inward, far_out = fence(
        kv_swapped, query_sums, backs, out_inward, far_out
    )
    out_passed = [add_inward(far_out[m], out_inward[m]) for m in range(micro)]
    query_sums = dp_sum_first(query_sums)
    kv_chip = plus(kv_parts[:, 0], kv_swapped).reshape(n_line, flat, lanes)
    half = n_line // 2
    kv_near_part = kv_chip[:half].reshape(half * flat, lanes)
    kv_far_part = kv_chip[half:].reshape(half * flat, lanes)
    kv_passed = add_inward(kv_far_part, sum_inward(kv_far_part))
    kv_grad = sum_last(*sum_across(kv_near_part, kv_passed)).astype(LOW)
    kv_grad, query_sums, out_sum, out_passed = fence(kv_grad, query_sums, out_sum, out_passed)
    both = dp_sum_second(query_sums).astype(LOW)
    out_half = out_sum.shape[0] // 2
    out_crossed = [sum_across(near_out[0], out_passed[0])]
    kv_sum = contract(normed.reshape(flat, width), kv_grad, 0, 0).astype(LOW)
    kv_sum = kv_sum.reshape(n_dp, n_line, 2, kv_part, lanes)
    kv_mine = lax.dynamic_index_in_dim(kv_sum, core, 2, keepdims=False)
    kv_theirs = lax.dynamic_index_in_dim(kv_sum, 1 - core, 2, keepdims=False)
    kv_sum = plus(kv_mine, swap_core(kv_theirs))
    kv_sum = jnp.concatenate(
        [lax.dynamic_slice_in_dim(kv_sum, spot, 1, 1) for spot in order], axis=1
    ).reshape(n_dp, -1, query_cols)
    kv_sums = dp_sum_first([kv_sum[i] for i in range(n_dp)])
    both, kv_sums, kv_grad, out_passed, out_crossed, down_sum, out_sum = fence(
        both, kv_sums, kv_grad, out_passed, out_crossed, down_sum, out_sum
    )
    kv_sums = dp_sum_second(kv_sums).astype(LOW)
    out_weight_inward = sum_inward(out_sum[out_half:])
    out_crossed.append(sum_across(near_out[1], out_passed[1]))
    queries = both.reshape(n_line, query_size, query_cols)
    both = jnp.concatenate([queries, kv_sums.reshape(n_line, -1, query_cols)], axis=1)
    both_near = both[:half].reshape(-1, query_cols)
    both_far = both[half:].reshape(-1, query_cols)
    output_sums = [sum_last(*out_crossed[0])]
    both_near, both_far, kv_grad, down_sum = fence(both_near, both_far, kv_grad, down_sum)
    both_inward = sum_inward(both_far)
    down_weight_grad = dp_sum_second(down_sum)
    out_weight_sums = sum_across(
        out_sum[:out_half], add_inward(out_sum[out_half:], out_weight_inward)
    )
    input_grads = []
    gain_one_grad = shift_one_grad = query_bias_grad = 0.0
    out_bias_grad = down_bias_grad = 0.0
    for m in range(micro):
        mine, theirs = backs[m]
        grad_rows = (
            mine
            + theirs.astype(WIDE)
            + contract(kv_grad[m * rows : (m + 1) * rows], kv_full, 1, 1)
        )
        moved, gain_part, shift_part = norm_backward(tok_rows[m], gain_one, grad_rows)
        gain_one_grad = gain_one_grad + gain_part
        shift_one_grad = shift_one_grad + shift_part
        query_bias_grad = query_bias_grad + jnp.sum(query_grad[m].astype(WIDE), axis=0)
        out_bias_grad = out_bias_grad + jnp.sum(middle_low[m].astype(WIDE), axis=0)
        down_bias_grad = down_bias_grad + jnp.sum(cot_low[m].astype(WIDE), axis=0)
        input_grads.append(relative((middle_grad[m] + moved).astype(LOW), 1))
    gain_two_grad = sum(g for g, _ in norm_two_grads)
    shift_two_grad = sum(g for _, g in norm_two_grads)
    value_bias_grad = jnp.sum(kv_grad[:, HD:].astype(WIDE), axis=0)
    up_bias_grad = sum(jnp.sum(p.astype(WIDE), axis=0) for p in pre_grad)
    both_inward, both_far, out_weight_sums, out_crossed, gain_one_grad, up_bias_grad = fence(
        both_inward, both_far, out_weight_sums, out_crossed, gain_one_grad, up_bias_grad
    )
    both_crossed = sum_across(both_near, add_inward(both_far, both_inward))
    out_weight_grad = sum_last(*out_weight_sums)
    output_sums.append(sum_last(*out_crossed[1]))
    (both_crossed,) = fence(both_crossed)
    both = sum_last(*both_crossed)
    query_weight_grad = both[:query_size]
    kv_weight_grad = both[query_size:].reshape(kv_part, lanes)
    outputs = []
    for m in range(micro):
        outputs.append(relative((middle[m] + down_shift + output_sums[m]).astype(LOW), 1))

    def by_owner(vector):
        return vector.reshape(n_dp, n_mp, -1)

    query_table_grad = query_bias_grad.reshape(n_line, heads_part * HD)
    cells = query_table_grad.reshape(n_line, 1, heads_part * HD)
    spots = jnp.arange(n_line, dtype=jnp.int32)[:, None]
    query_table_grad = sum(
        jnp.where(spots == place, cells[i], 0.0) for i, place in enumerate(order)
    ).reshape(n_line, heads_part, n_dp, slim)
    query_table_grad = query_table_grad.transpose(2, 0, 1, 3)
    query_table_grad = relative(query_table_grad, 0).reshape(n_dp, n_line, 1, heads_part * slim)
    sides = jnp.arange(2, dtype=jnp.int32)[None, None, :, None]
    query_table_grad = jnp.where(sides == core, query_table_grad, 0.0)
    up_table_grad = up_bias_grad.reshape(units_part, n_dp, slim).transpose(1, 0, 2)
    up_table_grad = relative(up_table_grad, 0).reshape(n_dp, 1, units_part * slim)
    places = jnp.arange(n_mp, dtype=jnp.int32)[None, :, None]
    up_table_grad = jnp.where(places == mp, up_table_grad, 0.0)
    value_table_grad = relative(value_bias_grad.reshape(n_dp, n_mp, -1), 0)
    parts = jnp.concatenate(
        [
            by_owner(gain_one_grad),
            by_owner(shift_one_grad),
            by_owner(out_bias_grad),
            by_owner(gain_two_grad),
            by_owner(shift_two_grad),
            by_owner(down_bias_grad),
            value_table_grad,
            query_table_grad.reshape(n_dp, n_mp, -1),
            up_table_grad,
        ],
        axis=2,
    )
    mine = pack_reduce(fence(parts, both_crossed)[0])
    at = 6 * part
    value_size = value_bias.shape[0]
    query_cells = heads_part * slim
    return (
        jnp.stack(outputs),
        jnp.stack(input_grads),
        mine[:part],
        mine[part : 2 * part],
        query_weight_grad,
        mine[at + value_size : at + value_size + query_cells].reshape(heads_part, slim),
        kv_weight_grad,
        mine[at : at + value_size],
        out_weight_grad,
        mine[2 * part : 3 * part],
        mine[3 * part : 4 * part],
        mine[4 * part : 5 * part],
        up_weight_grad,
        mine[at + value_size + query_cells :].reshape(units_part, slim),
        down_weight_grad,
        mine[5 * part : 6 * part],
    )


def solution(mesh):
    both = ("dp", "mp")
    in_specs = (
        P(None, both, None),
        P(None, "dp"),
        P(None, both, None),
        P(both),
        P(both),
        P("dp", "mp"),
        P("mp", "dp"),
        P(both, None),
        P(both),
        P("mp", "dp"),
        P(both),
        P(both),
        P(both),
        P("dp", "mp"),
        P("mp", "dp"),
        P("mp", "dp"),
        P(both),
    )
    out_specs = (
        P(None, both, None),
        P(None, both, None),
        P(both),
        P(both),
        P("dp", "mp"),
        P("mp", "dp"),
        P(both, None),
        P(both),
        P("mp", "dp"),
        P(both),
        P(both),
        P(both),
        P("dp", "mp"),
        P("mp", "dp"),
        P("mp", "dp"),
        P(both),
    )
    return jax.shard_map(
        on_device, mesh=mesh, in_specs=in_specs, out_specs=out_specs, check_vma=False
    )
```

time: 1720 us -> 686 us (0.40)
  waiting for transfers between devices: 1230 us -> 198 us
  matrix products: 237 us -> 13.3 us
  starting transfers between devices: 3.78 us -> 156 us
  Pallas kernels: 0 us -> 122 us
  blocking collectives: 99.4 us -> 0 us
  other arithmetic: 68.1 us -> 103 us
  local copies, waits for them, and re-layouts: 44.4 us -> 66 us
    reduce_scatter x19 -> x0, waiting for transfers between devices: 789 us -> none  [the longest x2 104 us: reduce_layer(): lax.psum_scatter(grad_parts[5].astype(jnp.bfloat16), 'dp', scatter_dimens...]
    all_gather x13 -> x1, waiting for transfers between devices: 387 us -> 4.25 us  [on_device(): lax.all_gather(jnp.concatenate([kv_weight, table], axis=0), ('dp', 'mp'),...]
    ppermute x0 -> x113, waiting for transfers between devices: none -> 194 us  [the longest x38 92.3 us: swap_dp(): return lax.ppermute(block, 'dp', [(i, i ^ bit) for i in range(count)])]
    ppermute x0 -> x113, starting transfers between devices: none -> 156 us  [the longest x17 46.5 us: swap_mp(): return lax.ppermute(block, 'mp', [(i, i ^ bit) for i in range(count)])]
    pallas_call x0 -> x12, Pallas kernels: none -> 122 us  [the longest x4 44.8 us: mlp(): pl.pallas_call(lambda *refs: mlp_kernel(n, *refs), out_shape=[shaped((2 *...]
    dot_general x38 -> x0, matrix products: 121 us -> none  [the longest x2 21 us: on_device(): jnp.dot(hidden, down_full, preferred_element_type=jnp.float32)]
    dot_general x20 -> x8, matrix products: 117 us -> 13.3 us  [contract(): lax.dot_general(left, right, (((left_dim,), (right_dim,)), ((), ())), pre...]
    unnamed x2 -> x0, blocking collectives: 81.8 us -> none
  transfers between devices with their start and end apart: 36 -> 114, of which waited for: 33 -> 39; matrix products, arithmetic and copies ran while one was open for 17% -> 22% of each run, Pallas kernels for 0% -> 18%
where the time goes in v1:
time: 686 us; the launch traced here: 676 us
  waiting for transfers between devices  198 us (29%)
  starting transfers between devices  156 us (23%)
  Pallas kernels  122 us (18%)
  other arithmetic  103 us (15%)
  local copies, waits for them, and re-layouts  66 us (10%)
  between operations  18.1 us (3%)
  matrix products  13.3 us (2%)
    ppermute x38, waiting for transfers between devices, swap_dp(): return lax.ppermute(block, 'dp', [(i, i ^ bit) for i in range(count)])  92.3 us
    ppermute x17, starting transfers between devices, swap_mp(): return lax.ppermute(block, 'mp', [(i, i ^ bit) for i in range(count)])  46.5 us
    pallas_call x4, Pallas kernels, mlp(): pl.pallas_call(lambda *refs: mlp_kernel(n, *refs), out_shape=[shaped((2 *...  44.8 us
    ppermute x38, starting transfers between devices, swap_dp(): return lax.ppermute(block, 'dp', [(i, i ^ bit) for i in range(count)])  38.6 us
    convert_element_type x25, other arithmetic, plus(): return (left.astype(WIDE) + right.astype(WIDE)).astype(LOW)  37.2 us
    ppermute x9, starting transfers between devices, move_in(): return lax.ppermute(block, 'mp', line_pairs([(0, 1), (3, 2)]))  35.4 us
    ppermute x5, waiting for transfers between devices, line_out(): outward = lax.ppermute(across, 'mp', line_pairs([(1, 0), (2, 3)]))  34.5 us
    ppermute x17, waiting for transfers between devices, swap_mp(): return lax.ppermute(block, 'mp', [(i, i ^ bit) for i in range(count)])  32.3 us
  transfers between devices with their start and end apart: 114, of which 39 were waited for; matrix products, arithmetic and copies ran while one was open for 22% of the time, Pallas kernels for 18%

profile of v1, /device:TPU:0, one launch (start us, length us, event | category | flops | bytes accessed | tf_op | source)
XLA Modules:
  0.0 676.4 jit_solution(17717779247451895545)
XLA Ops:
  36.4 8.3 %collective-permute-done.3 = bf16[128,2048]{1,0:T(8,128)(2,1)S(1)} collective-permute-done((bf16[128,2048]{1,0:T(8,128)(2,1)S(1)}, bf16[128,2048]{1,0:T(8,128)(2,1)S(1)}, u32[]{:S(2)}, u32[]{:S(2)}) %collective-permute-start.3) | collective-permute-done | bytes 524320 | tf_op jit(solution)/shard_map/ppermute | solution.py:71
  57.5 10.3 %collective-permute-done.6 = bf16[1024,256]{1,0:T(8,128)(2,1)S(1)} collective-permute-done((bf16[1024,256]{1,0:T(8,128)(2,1)S(1)}, bf16[1024,256]{1,0:T(8,128)(2,1)S(1)}, u32[]{:S(2)}, u32[]{:S(2)}) %collective-permute-start.6) | collective-permute-done | bytes 524320 | tf_op jit(solution)/shard_map/ppermute | solution.py:108
  93.0 8.6 %collective-permute-start.16 = (bf16[256,256]{1,0:T(8,128)(2,1)S(1)}, bf16[256,256]{1,0:T(8,128)(2,1)S(1)}, u32[]{:S(2)}, u32[]{:S(2)}) collective-permute-start(bf16[256,256]{1,0:T(8,128)(2,1)S(1)} %fusion.16), channel_id=1, source_target_pairs={{0,2},{1,3},{2,0},{3,1},{4,6},{5,7},{6,4},{7,5},{8,10},{9,11},{10,... | collective-permute-start | bytes 393224 | tf_op jit(solution)/shard_map/ppermute | solution.py:71
  136.6 9.3 %shard_map.289 = (bf16[8,256,128]{2,1,0:T(8,128)(2,1)S(1)}, bf16[256,1024]{1,0:T(8,128)(2,1)S(1)}, bf16[8,256,1024]{2,1,0:T(8,128)(2,1)S(1)}) custom-call(bf16[128,2048]{1,0:T(8,128)(2,1)S(1)} %get-tuple-element.696.refs_0_, bf16[128,2048]{1,0:T(8,128)(2,1)S(1)} %get-tuple-element.706.refs_1_, ...), custom_call_target="tpu_custom_call" | custom-call | flops 2147483648 | bytes 8388608 | tf_op jit(solution)/shard_map/pallas_call | solution.py:352
  147.9 9.3 %shard_map.288 = (bf16[8,256,128]{2,1,0:T(8,128)(2,1)S(1)}, bf16[256,1024]{1,0:T(8,128)(2,1)S(1)}, bf16[8,256,1024]{2,1,0:T(8,128)(2,1)S(1)}) custom-call(bf16[128,2048]{1,0:T(8,128)(2,1)S(1)} %get-tuple-element.697.refs_0_, bf16[128,2048]{1,0:T(8,128)(2,1)S(1)} %get-tuple-element.707.refs_1_, ...), custom_call_target="tpu_custom_call" | custom-call | flops 2147483648 | bytes 8388608 | tf_op jit(solution)/shard_map/pallas_call | solution.py:352
  162.7 11.5 %collective-permute-done.27 = bf16[512,512]{1,0:T(8,128)(2,1)S(1)} collective-permute-done((bf16[512,512]{1,0:T(8,128)(2,1)S(1)}, bf16[512,512]{1,0:T(8,128)(2,1)S(1)}, u32[]{:S(2)}, u32[]{:S(2)}) %collective-permute-start.27) | collective-permute-done | bytes 524320 | tf_op jit(solution)/shard_map/ppermute | solution.py:66
  188.8 6.7 collective-permute-start.31
  197.0 18.1 %collective-permute-done.35 = bf16[256,2048]{1,0:T(8,128)(2,1)S(1)} collective-permute-done((bf16[256,2048]{1,0:T(8,128)(2,1)}, bf16[256,2048]{1,0:T(8,128)(2,1)S(1)}, u32[]{:S(2)}, u32[]{:S(2)}) %collective-permute-start.35) | collective-permute-done | bytes 1048608 | tf_op jit(solution)/shard_map/ppermute | solution.py:108
  216.4 9.4 %collective-permute-done.31 = bf16[128,2048]{1,0:T(8,128)(2,1)} collective-permute-done((bf16[128,2048]{1,0:T(8,128)(2,1)S(1)}, bf16[128,2048]{1,0:T(8,128)(2,1)}, u32[]{:S(2)}, u32[]{:S(2)}) %collective-permute-start.31) | collective-permute-done | bytes 524320 | tf_op jit(solution)/shard_map/ppermute | solution.py:71
  232.6 10.6 %collective-permute-done.39 = bf16[512,512]{1,0:T(8,128)(2,1)S(1)} collective-permute-done((bf16[512,512]{1,0:T(8,128)(2,1)S(1)}, bf16[512,512]{1,0:T(8,128)(2,1)S(1)}, u32[]{:S(2)}, u32[]{:S(2)}) %collective-permute-start.39) | collective-permute-done | bytes 524320 | tf_op jit(solution)/shard_map/ppermute | solution.py:66
  248.9 10.8 %shard_map.292 = (bf16[512,1024]{1,0:T(8,128)(2,1)S(1)}, bf16[512,1024]{1,0:T(8,128)(2,1)S(1)}, bf16[256,2048]{1,0:T(8,128)(2,1)S(1)}, bf16[256,2048]{1,0:T(8,128)(2,1)S(1)}, bf16[512,2048]{1,0:T(8,128)(2,1)S(1)}) custom-call(bf16[256,2048]{1,0:T(8,128)(2,1)S(1)} %constant_dynamic-update-slice_fusion.5.refs_0_, ...), custom_call_target="tpu_custom_call" | custom-call | flops 8589934592 | bytes 16777216 | tf_op jit(solution)/shard_map/pallas_call | solution.py:534
  269.6 10.8 %shard_map.293 = (bf16[512,1024]{1,0:T(8,128)(2,1)S(1)}, bf16[512,1024]{1,0:T(8,128)(2,1)S(1)}, bf16[256,2048]{1,0:T(8,128)(2,1)S(1)}, bf16[256,2048]{1,0:T(8,128)(2,1)S(1)}, bf16[512,2048]{1,0:T(8,128)(2,1)S(1)}) custom-call(bf16[256,2048]{1,0:T(8,128)(2,1)S(1)} %pad_maximum_fusion.11.refs_0_.refs_2_, ...), custom_call_target="tpu_custom_call" | custom-call | flops 8589934592 | bytes 16777216 | tf_op jit(solution)/shard_map/pallas_call | solution.py:534
  286.5 14.4 %collective-permute-done.49 = bf16[128,2048]{1,0:T(8,128)(2,1)S(1)} collective-permute-done((bf16[128,2048]{1,0:T(8,128)(2,1)S(1)}, bf16[128,2048]{1,0:T(8,128)(2,1)S(1)}, u32[]{:S(2)}, u32[]{:S(2)}) %collective-permute-start.49) | collective-permute-done | bytes 524320 | tf_op jit(solution)/shard_map/ppermute | solution.py:118
  306.3 11.9 %shard_map.294 = (bf16[512,1024]{1,0:T(8,128)(2,1)S(1)}, bf16[512,1024]{1,0:T(8,128)(2,1)S(1)}, bf16[256,2048]{1,0:T(8,128)(2,1)S(1)}, bf16[256,2048]{1,0:T(8,128)(2,1)S(1)}, bf16[512,2048]{1,0:T(8,128)(2,1)}) custom-call(bf16[256,2048]{1,0:T(8,128)(2,1)S(1)} %constant_dynamic-update-slice_fusion.7.refs_0_.refs_4_, ...), custom_call_target="tpu_custom_call" | custom-call | flops 8589934592 | bytes 16777216 | tf_op jit(solution)/shard_map/pallas_call | solution.py:534
  341.4 11.2 %shard_map.295 = (bf16[512,1024]{1,0:T(8,128)(2,1)S(1)}, bf16[512,1024]{1,0:T(8,128)(2,1)S(1)}, bf16[256,2048]{1,0:T(8,128)(2,1)S(1)}, bf16[256,2048]{1,0:T(8,128)(2,1)S(1)}, bf16[512,2048]{1,0:T(8,128)(2,1)S(1)}) custom-call(bf16[256,2048]{1,0:T(8,128)(2,1)S(1)} %copy-done.34, bf16[256,2048]{1,0:T(8,128)(2,1)} %collective-permute-done.58.refs_1_.refs_7_, ...), custom_call_target="tpu_custom_call" | custom-call | flops 8589934592 | bytes 16777216 | tf_op jit(solution)/shard_map/pallas_call | solution.py:534
  358.1 13.0 %shard_map.296 = bf16[4,512,1024]{2,1,0:T(8,128)(2,1)} custom-call(bf16[256,2048]{1,0:T(8,128)(2,1)S(1)} %copy-done.53, bf16[256,2048]{1,0:T(8,128)(2,1)S(1)} %copy-done.67, bf16[256,2048]{1,0:T(8,128)(2,1)S(1)} %copy-done.27, bf16[256,2048]{1,0:T(8,128)(2,1)S(1)} %copy-done.71, bf16[256,2048]{1,0:T(8,128)(2,1)S(1)} %copy-done.55, ...), custom_call_target="tpu_custom_call" | custom-call | flops 8589934592 | bytes 16777216 | tf_op jit(solution)/shard_map/pallas_call | solution.py:565
  408.6 13.8 %shard_map.297 = (bf16[256,1024]{1,0:T(8,128)(2,1)S(1)}, bf16[1024,256]{1,0:T(8,128)(2,1)S(1)}, f32[128,2048]{1,0:T(8,128)S(1)}, bf16[128,2048]{1,0:T(8,128)(2,1)S(1)}) custom-call(bf16[128,2048]{1,0:T(8,128)(2,1)S(1)} %get-tuple-element.521.refs_0_, bf16[128,2048]{1,0:T(8,128)(2,1)S(1)} %collective-permute-done.65.refs_1_, ...), custom_call_target="tpu_custom_call" | custom-call | flops 4294967296 | bytes 12582912 | tf_op jit(solution)/shard_map/pallas_call | solution.py:464
  430.2 13.5 %shard_map.298 = bf16[4,1024,512]{2,1,0:T(8,128)(2,1)} custom-call(bf16[512,1024]{1,0:T(8,128)(2,1)S(1)} %copy-done.83, bf16[512,1024]{1,0:T(8,128)(2,1)S(1)} %copy-done.85, bf16[512,1024]{1,0:T(8,128)(2,1)S(1)} %copy-done.87, bf16[512,1024]{1,0:T(8,128)(2,1)S(1)} %get-tuple-element.507.refs_3_, bf16[256,2048]{1,0:T(8,128)(2,1)} %pad_maximum_fusion.3.refs_2_.refs_4_, ...), custom_call_target="tpu_custom_call" | custom-call | flops 8589934592 | bytes 16777216 | tf_op jit(solution)/shard_map/pallas_call | solution.py:604
  479.8 13.9 %shard_map.299 = (bf16[256,1024]{1,0:T(8,128)(2,1)S(1)}, bf16[1024,256]{1,0:T(8,128)(2,1)S(1)}, f32[128,2048]{1,0:T(8,128)S(1)}, bf16[128,2048]{1,0:T(8,128)(2,1)S(1)}) custom-call(bf16[128,2048]{1,0:T(8,128)(2,1)S(1)} %get-tuple-element.528.refs_0_, bf16[128,2048]{1,0:T(8,128)(2,1)S(1)} %collective-permute-done.73.refs_1_, ...), custom_call_target="tpu_custom_call" | custom-call | flops 4294967296 | bytes 12582912 | tf_op jit(solution)/shard_map/pallas_call | solution.py:464
  517.8 7.8 %collective-permute-start.84 = (bf16[256,256]{1,0:T(8,128)(2,1)S(1)}, bf16[256,256]{1,0:T(8,128)(2,1)S(1)}, u32[]{:S(2)}, u32[]{:S(2)}) collective-permute-start(bf16[256,256]{1,0:T(8,128)(2,1)S(1)} %fusion.74), channel_id=1, source_target_pairs={{0,2},{1,3},{2,0},{3,1},{4,6},{5,7},{6,4},{7,5},{8,10},{9,11},{10,... | collective-permute-start | bytes 393224 | tf_op jit(solution)/shard_map/ppermute | solution.py:71
  525.6 12.0 %collective-permute-done.86 = bf16[1024,256]{1,0:T(8,128)(2,1)S(1)} collective-permute-done((bf16[1024,256]{1,0:T(8,128)(2,1)S(1)}, bf16[1024,256]{1,0:T(8,128)(2,1)S(1)}, u32[]{:S(2)}, u32[]{:S(2)}) %collective-permute-start.86) | collective-permute-done | bytes 524320 | tf_op jit(solution)/shard_map/ppermute | solution.py:66
  551.6 21.7 %collective-permute-done.93 = bf16[128,256]{1,0:T(8,128)(2,1)S(1)} collective-permute-done((bf16[128,256]{1,0:T(8,128)(2,1)S(1)}, bf16[128,256]{1,0:T(8,128)(2,1)S(1)}, u32[]{:S(2)}, u32[]{:S(2)}) %collective-permute-start.93) | collective-permute-done | bytes 65568 | tf_op jit(solution)/shard_map/ppermute | solution.py:66
  602.9 7.1 %collective-permute-start.98 = (bf16[1152,256]{1,0:T(8,128)(2,1)}, bf16[1152,256]{1,0:T(8,128)(2,1)S(1)}, u32[]{:S(2)}, u32[]{:S(2)}) collective-permute-start(bf16[1152,256]{1,0:T(8,128)(2,1)} %bitcast.84), channel_id=1, source_target_pairs={{0,2},{1,3},{6,4},{7,5},{8,10},{9,11},{14,12},{15,13},{16,18},{17,... | collective-permute-start | bytes 1769480 | tf_op jit(solution)/shard_map/ppermute | solution.py:122
  614.4 6.9 %collective-permute-done.98 = bf16[1152,256]{1,0:T(8,128)(2,1)S(1)} collective-permute-done((bf16[1152,256]{1,0:T(8,128)(2,1)}, bf16[1152,256]{1,0:T(8,128)(2,1)S(1)}, u32[]{:S(2)}, u32[]{:S(2)}) %collective-permute-start.98) | collective-permute-done | bytes 589856 | tf_op jit(solution)/shard_map/ppermute | solution.py:122
  (902 shorter events, 387.4 us)
Async XLA Ops:
  7.2 69.3 %all-gather.2.cloned.1.call-start = ((), (), s32[]{:S(2)}) async-start(), calls=%async_computation | async-start | bytes 1351680 | tf_op jit(solution)/shard_map/all_gather | solution.py:660
  7.2 38.5 %collective-permute-start.4 = (bf16[512,1024]{1,0:T(8,128)(2,1)}, bf16[512,1024]{1,0:T(8,128)(2,1)S(1)}, u32[]{:S(2)}, u32[]{:S(2)}) collective-permute-start(bf16[512,1024]{1,0:T(8,128)(2,1)} %refs_4_.3), channel_id=1, source_target_pairs={{0,8},{8,0},{16,24},{24,16},{1,9},{9,1},{17,25},{25,17},{2,10},{10... | collective-permute-start | bytes 3145736 | tf_op jit(solution)/shard_map/ppermute | solution.py:66
  10.2 35.5 %collective-permute-start.5 = (bf16[512,1024]{1,0:T(8,128)(2,1)}, bf16[512,1024]{1,0:T(8,128)(2,1)S(1)}, u32[]{:S(2)}, u32[]{:S(2)}) collective-permute-start(bf16[512,1024]{1,0:T(8,128)(2,1)} %refs_4_.3), channel_id=1, source_target_pairs={{0,16},{8,24},{16,0},{24,8},{1,17},{9,25},{17,1},{25,9},{2,18},{10... | collective-permute-start | bytes 3145736 | tf_op jit(solution)/shard_map/ppermute | solution.py:66
  31.2 50.9 %collective-permute-start.15 = (bf16[128,2048]{1,0:T(8,128)(2,1)}, bf16[128,2048]{1,0:T(8,128)(2,1)}, u32[]{:S(2)}, u32[]{:S(2)}) collective-permute-start(bf16[128,2048]{1,0:T(8,128)(2,1)} %get-tuple-element.710), channel_id=1, source_target_pairs={{0,2},{1,3},{2,0},{3,1},{4,6},{5,7},{6,4},{7,5},{8,10},{9,11},{10,... | collective-permute-start | bytes 1572872 | tf_op jit(solution)/shard_map/ppermute | solution.py:71
  129.6 29.5 %collective-permute-start.25 = (bf16[256,2048]{1,0:T(8,128)(2,1)}, bf16[256,2048]{1,0:T(8,128)(2,1)S(1)}, u32[]{:S(2)}, u32[]{:S(2)}) collective-permute-start(bf16[256,2048]{1,0:T(8,128)(2,1)} %collective-permute-done.14), channel_id=1, source_target_pairs={{2,0},{3,1},{4,6},{5,7},{10,8},{11,9},{12,14},{13,15},{18,16},{19,... | collective-permute-start | bytes 3145736 | tf_op jit(solution)/shard_map/ppermute | solution.py:108
  182.9 32.2 %collective-permute-start.35 = (bf16[256,2048]{1,0:T(8,128)(2,1)}, bf16[256,2048]{1,0:T(8,128)(2,1)S(1)}, u32[]{:S(2)}, u32[]{:S(2)}) collective-permute-start(bf16[256,2048]{1,0:T(8,128)(2,1)} %copy-done.140), channel_id=1, source_target_pairs={{2,0},{3,1},{4,6},{5,7},{10,8},{11,9},{12,14},{13,15},{18,16},{19,... | collective-permute-start | bytes 3145736 | tf_op jit(solution)/shard_map/ppermute | solution.py:108
  184.2 32.3 %collective-permute-start.33 = (bf16[1024,512]{1,0:T(8,128)(2,1)}, bf16[1024,512]{1,0:T(8,128)(2,1)}, u32[]{:S(2)}, u32[]{:S(2)}) collective-permute-start(bf16[1024,512]{1,0:T(8,128)(2,1)} %refs_8_.3), channel_id=1, source_target_pairs={{0,8},{8,0},{16,24},{24,16},{1,9},{9,1},{17,25},{25,17},{2,10},{10... | collective-permute-start | bytes 3145736 | tf_op jit(solution)/shard_map/ppermute | solution.py:66
  184.6 31.8 %collective-permute-start.34 = (bf16[1024,512]{1,0:T(8,128)(2,1)}, bf16[1024,512]{1,0:T(8,128)(2,1)}, u32[]{:S(2)}, u32[]{:S(2)}) collective-permute-start(bf16[1024,512]{1,0:T(8,128)(2,1)} %refs_8_.3), channel_id=1, source_target_pairs={{0,16},{8,24},{16,0},{24,8},{1,17},{9,25},{17,1},{25,9},{2,18},{10... | collective-permute-start | bytes 3145736 | tf_op jit(solution)/shard_map/ppermute | solution.py:66
  188.8 37.0 %collective-permute-start.31 = (bf16[128,2048]{1,0:T(8,128)(2,1)S(1)}, bf16[128,2048]{1,0:T(8,128)(2,1)}, u32[]{:S(2)}, u32[]{:S(2)}) collective-permute-start(bf16[128,2048]{1,0:T(8,128)(2,1)S(1)} %get-tuple-element.371), channel_id=1, source_target_pairs={{0,2},{1,3},{2,0},{3,1},{4,6},{5,7},{6,4},{7,5},{8,10},{9,11},{10,... | collective-permute-start | bytes 1572872 | tf_op jit(solution)/shard_map/ppermute | solution.py:71
  195.5 30.3 %collective-permute-start.32 = (bf16[128,2048]{1,0:T(8,128)(2,1)S(1)}, bf16[128,2048]{1,0:T(8,128)(2,1)}, u32[]{:S(2)}, u32[]{:S(2)}) collective-permute-start(bf16[128,2048]{1,0:T(8,128)(2,1)S(1)} %get-tuple-element.371), channel_id=1, source_target_pairs={{2,4},{3,5},{4,2},{5,3},{10,12},{11,13},{12,10},{13,11},{18,20},{1... | collective-permute-start | bytes 1572872 | tf_op jit(solution)/shard_map/ppermute | solution.py:114
  322.4 30.3 %collective-permute-start.57 = (bf16[512,2048]{1,0:T(8,128)(2,1)}, bf16[512,2048]{1,0:T(8,128)(2,1)}, u32[]{:S(2)}, u32[]{:S(2)}) collective-permute-start(bf16[512,2048]{1,0:T(8,128)(2,1)} %get-tuple-element.438), channel_id=1, source_target_pairs={{0,1},{1,0},{2,3},{3,2},{4,5},{5,4},{6,7},{7,6},{8,9},{9,8},{10,11... | collective-permute-start | bytes 6291464 | tf_op jit(solution)/shard_map/ppermute | solution.py:56
  399.5 44.2 %collective-permute-start.71 = (bf16[512,1024]{1,0:T(8,128)(2,1)}, bf16[512,1024]{1,0:T(8,128)(2,1)S(1)}, u32[]{:S(2)}, u32[]{:S(2)}) collective-permute-start(bf16[512,1024]{1,0:T(8,128)(2,1)} %pad_maximum_fusion.13), channel_id=1, source_target_pairs={{0,8},{8,0},{16,24},{24,16},{1,9},{9,1},{17,25},{25,17},{2,10},{10... | collective-permute-start | bytes 3145736 | tf_op jit(solution)/shard_map/ppermute | solution.py:66
  401.2 42.5 %collective-permute-start.72 = (bf16[512,1024]{1,0:T(8,128)(2,1)}, bf16[512,1024]{1,0:T(8,128)(2,1)S(1)}, u32[]{:S(2)}, u32[]{:S(2)}) collective-permute-start(bf16[512,1024]{1,0:T(8,128)(2,1)} %pad_maximum_fusion.14), channel_id=1, source_target_pairs={{0,16},{8,24},{16,0},{24,8},{1,17},{9,25},{17,1},{25,9},{2,18},{10... | collective-permute-start | bytes 3145736 | tf_op jit(solution)/shard_map/ppermute | solution.py:66
  453.1 50.2 %collective-permute-start.80 = (bf16[256,2048]{1,0:T(8,128)(2,1)}, bf16[256,2048]{1,0:T(8,128)(2,1)}, u32[]{:S(2)}, u32[]{:S(2)}) collective-permute-start(bf16[256,2048]{1,0:T(8,128)(2,1)} %add_convert_fusion.10), channel_id=1, source_target_pairs={{0,2},{1,3},{6,4},{7,5},{8,10},{9,11},{14,12},{15,13},{16,18},{17,... | collective-permute-start | bytes 3145736 | tf_op jit(solution)/shard_map/ppermute | solution.py:122
  473.3 31.8 %collective-permute-start.81 = (bf16[256,2048]{1,0:T(8,128)(2,1)}, bf16[256,2048]{1,0:T(8,128)(2,1)}, u32[]{:S(2)}, u32[]{:S(2)}) collective-permute-start(bf16[256,2048]{1,0:T(8,128)(2,1)} %add_convert_fusion.6), channel_id=1, source_target_pairs={{0,2},{1,3},{6,4},{7,5},{8,10},{9,11},{14,12},{15,13},{16,18},{17,... | collective-permute-start | bytes 3145736 | tf_op jit(solution)/shard_map/ppermute | solution.py:122
  501.2 38.5 %collective-permute-start.87 = (bf16[1024,512]{1,0:T(8,128)(2,1)S(1)}, bf16[1024,512]{1,0:T(8,128)(2,1)S(1)}, u32[]{:S(2)}, u32[]{:S(2)}) collective-permute-start(bf16[1024,512]{1,0:T(8,128)(2,1)S(1)} %pad_maximum_fusion.17), channel_id=1, source_target_pairs={{0,8},{8,0},{16,24},{24,16},{1,9},{9,1},{17,25},{25,17},{2,10},{10... | collective-permute-start | bytes 3145736 | tf_op jit(solution)/shard_map/ppermute | solution.py:66
  503.4 36.3 %collective-permute-start.88 = (bf16[1024,512]{1,0:T(8,128)(2,1)S(1)}, bf16[1024,512]{1,0:T(8,128)(2,1)S(1)}, u32[]{:S(2)}, u32[]{:S(2)}) collective-permute-start(bf16[1024,512]{1,0:T(8,128)(2,1)S(1)} %pad_maximum_fusion.18), channel_id=1, source_target_pairs={{0,16},{8,24},{16,0},{24,8},{1,17},{9,25},{17,1},{25,9},{2,18},{10... | collective-permute-start | bytes 3145736 | tf_op jit(solution)/shard_map/ppermute | solution.py:66
  505.2 32.4 %collective-permute-start.86 = (bf16[1024,256]{1,0:T(8,128)(2,1)S(1)}, bf16[1024,256]{1,0:T(8,128)(2,1)S(1)}, u32[]{:S(2)}, u32[]{:S(2)}) collective-permute-start(bf16[1024,256]{1,0:T(8,128)(2,1)S(1)} %get-tuple-element.704), channel_id=1, source_target_pairs={{0,8},{8,0},{16,24},{24,16},{1,9},{9,1},{17,25},{25,17},{2,10},{10... | collective-permute-start | bytes 1572872 | tf_op jit(solution)/shard_map/ppermute | solution.py:66
  505.6 33.9 %collective-permute-start.85 = (bf16[1024,256]{1,0:T(8,128)(2,1)S(1)}, bf16[1024,256]{1,0:T(8,128)(2,1)S(1)}, u32[]{:S(2)}, u32[]{:S(2)}) collective-permute-start(bf16[1024,256]{1,0:T(8,128)(2,1)S(1)} %get-tuple-element.705), channel_id=1, source_target_pairs={{0,16},{8,24},{16,0},{24,8},{1,17},{9,25},{17,1},{25,9},{2,18},{10... | collective-permute-start | bytes 1572872 | tf_op jit(solution)/shard_map/ppermute | solution.py:66
  545.3 28.7 %collective-permute-start.94 = (bf16[256,2048]{1,0:T(8,128)(2,1)}, bf16[256,2048]{1,0:T(8,128)(2,1)S(1)}, u32[]{:S(2)}, u32[]{:S(2)}) collective-permute-start(bf16[256,2048]{1,0:T(8,128)(2,1)} %add_convert_fusion.4), channel_id=1, source_target_pairs={{2,4},{3,5},{4,2},{5,3},{10,12},{11,13},{12,10},{13,11},{18,20},{1... | collective-permute-start | bytes 3145736 | tf_op jit(solution)/shard_map/ppermute | solution.py:114
  546.0 29.5 %collective-permute-start.89 = (bf16[2048,256]{1,0:T(8,128)(2,1)}, bf16[2048,256]{1,0:T(8,128)(2,1)S(1)}, u32[]{:S(2)}, u32[]{:S(2)}) collective-permute-start(bf16[2048,256]{1,0:T(8,128)(2,1)} %pad_maximum_fusion.23), channel_id=1, source_target_pairs={{0,8},{8,0},{16,24},{24,16},{1,9},{9,1},{17,25},{25,17},{2,10},{10... | collective-permute-start | bytes 3145736 | tf_op jit(solution)/shard_map/ppermute | solution.py:66
  586.3 47.3 %collective-permute-start.95 = (bf16[128,2048]{1,0:T(8,128)(2,1)}, bf16[128,2048]{1,0:T(8,128)(2,1)}, u32[]{:S(2)}, u32[]{:S(2)}) collective-permute-start(bf16[128,2048]{1,0:T(8,128)(2,1)} %get-tuple-element.572), channel_id=1, source_target_pairs={{0,2},{1,3},{2,0},{3,1},{4,6},{5,7},{6,4},{7,5},{8,10},{9,11},{10,... | collective-permute-start | bytes 1572872 | tf_op jit(solution)/shard_map/ppermute | solution.py:71
  587.5 40.5 %collective-permute-start.111 = (bf16[1024,512]{1,0:T(8,128)(2,1)}, bf16[1024,512]{1,0:T(8,128)(2,1)}, u32[]{:S(2)}, u32[]{:S(2)}) collective-permute-start(bf16[1024,512]{1,0:T(8,128)(2,1)} %pad_maximum_fusion.15), channel_id=1, source_target_pairs={{0,8},{8,0},{16,24},{24,16},{1,9},{9,1},{17,25},{25,17},{2,10},{10... | collective-permute-start | bytes 3145736 | tf_op jit(solution)/shard_map/ppermute | solution.py:66
  588.6 40.9 %collective-permute-start.112 = (bf16[1024,512]{1,0:T(8,128)(2,1)}, bf16[1024,512]{1,0:T(8,128)(2,1)}, u32[]{:S(2)}, u32[]{:S(2)}) collective-permute-start(bf16[1024,512]{1,0:T(8,128)(2,1)} %pad_maximum_fusion.16), channel_id=1, source_target_pairs={{0,16},{8,24},{16,0},{24,8},{1,17},{9,25},{17,1},{25,9},{2,18},{10... | collective-permute-start | bytes 3145736 | tf_op jit(solution)/shard_map/ppermute | solution.py:66
  (264 other events, 3046.1 us)
Sparse Core Ops, SparseCore 0:
  21.5 54.9 all-gather.1

commit v2 on v1

--- a/solution.py
+++ b/solution.py
@@ -944,19 +944,16 @@
         both, kv_sums, kv_grad, out_passed, out_crossed, down_sum, out_sum
     )
     kv_sums = dp_sum_second(kv_sums).astype(LOW)
-    out_weight_inward = sum_inward(out_sum[out_half:])
     out_crossed.append(sum_across(near_out[1], out_passed[1]))
     queries = both.reshape(n_line, query_size, query_cols)
     both = jnp.concatenate([queries, kv_sums.reshape(n_line, -1, query_cols)], axis=1)
     both_near = both[:half].reshape(-1, query_cols)
     both_far = both[half:].reshape(-1, query_cols)
-    output_sums = [sum_last(*out_crossed[0])]
-    both_near, both_far, kv_grad, down_sum = fence(both_near, both_far, kv_grad, down_sum)
+    both_near, both_far, kv_grad, down_sum, out_sum = fence(
+        both_near, both_far, kv_grad, down_sum, out_sum
+    )
     both_inward = sum_inward(both_far)
-    down_weight_grad = dp_sum_second(down_sum)
-    out_weight_sums = sum_across(
-        out_sum[:out_half], add_inward(out_sum[out_half:], out_weight_inward)
-    )
+    out_weight_inward = sum_inward(out_sum[out_half:])
     input_grads = []
     gain_one_grad = shift_one_grad = query_bias_grad = 0.0
     out_bias_grad = down_bias_grad = 0.0
@@ -978,13 +975,17 @@
     shift_two_grad = sum(g for _, g in norm_two_grads)
     value_bias_grad = jnp.sum(kv_grad[:, HD:].astype(WIDE), axis=0)
     up_bias_grad = sum(jnp.sum(p.astype(WIDE), axis=0) for p in pre_grad)
-    both_inward, both_far, out_weight_sums, out_crossed, gain_one_grad, up_bias_grad = fence(
-        both_inward, both_far, out_weight_sums, out_crossed, gain_one_grad, up_bias_grad
-    )
+    both_inward, both_far, down_sum, gain_one_grad, up_bias_grad, out_crossed, out_sum = fence(
+        both_inward, both_far, down_sum, gain_one_grad, up_bias_grad, out_crossed, out_sum
+    )
+    down_weight_grad = dp_sum_second(down_sum)
     both_crossed = sum_across(both_near, add_inward(both_far, both_inward))
+    out_weight_sums = sum_across(
+        out_sum[:out_half], add_inward(out_sum[out_half:], out_weight_inward)
+    )
+    both_crossed, out_crossed = fence(both_crossed, out_crossed)
+    output_sums = [sum_last(*crossed) for crossed in out_crossed]
     out_weight_grad = sum_last(*out_weight_sums)
-    output_sums.append(sum_last(*out_crossed[1]))
-    (both_crossed,) = fence(both_crossed)
     both = sum_last(*both_crossed)
     query_weight_grad = both[:query_size]
     kv_weight_grad = both[query_size:].reshape(kv_part, lanes)

time: 686 us -> 699 us (1.019)
  starting transfers between devices: 156 us -> 173 us
    ppermute x17, starting transfers between devices: 46.5 us -> 69.4 us  [swap_mp(): return lax.ppermute(block, 'mp', [(i, i ^ bit) for i in range(count)])]
    ppermute x9, waiting for transfers between devices: 11.9 us -> 4.08 us  [move_in(): return lax.ppermute(block, 'mp', line_pairs([(0, 1), (3, 2)]))]
    unnamed x358 -> x354, local copies, waits for them, and re-layouts: 20.9 us -> 21.7 us
  transfers between devices with their start and end apart: 114 -> 114, of which waited for: 39 -> 40; matrix products, arithmetic and copies ran while one was open for 22% -> 21% of each run, Pallas kernels for 18% -> 17%
where the time goes in v2:
time: 699 us; the launch traced here: 689 us
  waiting for transfers between devices  194 us (28%)
  starting transfers between devices  173 us (25%)
  Pallas kernels  122 us (17%)
  other arithmetic  104 us (15%)
  local copies, waits for them, and re-layouts  65.3 us (9%)
  between operations  18 us (3%)
  matrix products  13.3 us (2%)
    ppermute x38, waiting for transfers between devices, swap_dp(): return lax.ppermute(block, 'dp', [(i, i ^ bit) for i in range(count)])  92.1 us
    ppermute x17, starting transfers between devices, swap_mp(): return lax.ppermute(block, 'mp', [(i, i ^ bit) for i in range(count)])  69.4 us
    pallas_call x4, Pallas kernels, mlp(): pl.pallas_call(lambda *refs: mlp_kernel(n, *refs), out_shape=[shaped((2 *...  44.8 us
    ppermute x38, starting transfers between devices, swap_dp(): return lax.ppermute(block, 'dp', [(i, i ^ bit) for i in range(count)])  39.8 us
    convert_element_type x25, other arithmetic, plus(): return (left.astype(WIDE) + right.astype(WIDE)).astype(LOW)  37 us
    ppermute x17, waiting for transfers between devices, swap_mp(): return lax.ppermute(block, 'mp', [(i, i ^ bit) for i in range(count)])  35.9 us
    ppermute x5, waiting for transfers between devices, line_out(): outward = lax.ppermute(across, 'mp', line_pairs([(1, 0), (2, 3)]))  34.5 us
    ppermute x9, starting transfers between devices, move_in(): return lax.ppermute(block, 'mp', line_pairs([(0, 1), (3, 2)]))  29.3 us
  transfers between devices with their start and end apart: 114, of which 40 were waited for; matrix products, arithmetic and copies ran while one was open for 21% of the time, Pallas kernels for 17%

profile of v2, /device:TPU:0, one launch (start us, length us, event | category | flops | bytes accessed | tf_op | source)
XLA Modules:
  0.0 689.2 jit_solution(9308381266384040179)
XLA Ops:
  36.4 8.3 %collective-permute-done.3 = bf16[128,2048]{1,0:T(8,128)(2,1)S(1)} collective-permute-done((bf16[128,2048]{1,0:T(8,128)(2,1)S(1)}, bf16[128,2048]{1,0:T(8,128)(2,1)S(1)}, u32[]{:S(2)}, u32[]{:S(2)}) %collective-permute-start.3) | collective-permute-done | bytes 524320 | tf_op jit(solution)/shard_map/ppermute | solution.py:71
  57.5 10.3 %collective-permute-done.6 = bf16[1024,256]{1,0:T(8,128)(2,1)S(1)} collective-permute-done((bf16[1024,256]{1,0:T(8,128)(2,1)S(1)}, bf16[1024,256]{1,0:T(8,128)(2,1)S(1)}, u32[]{:S(2)}, u32[]{:S(2)}) %collective-permute-start.6) | collective-permute-done | bytes 524320 | tf_op jit(solution)/shard_map/ppermute | solution.py:108
  93.1 8.6 %collective-permute-start.16 = (bf16[256,256]{1,0:T(8,128)(2,1)S(1)}, bf16[256,256]{1,0:T(8,128)(2,1)S(1)}, u32[]{:S(2)}, u32[]{:S(2)}) collective-permute-start(bf16[256,256]{1,0:T(8,128)(2,1)S(1)} %fusion.16), channel_id=1, source_target_pairs={{0,2},{1,3},{2,0},{3,1},{4,6},{5,7},{6,4},{7,5},{8,10},{9,11},{10,... | collective-permute-start | bytes 393224 | tf_op jit(solution)/shard_map/ppermute | solution.py:71
  136.6 9.3 %shard_map.289 = (bf16[8,256,128]{2,1,0:T(8,128)(2,1)S(1)}, bf16[256,1024]{1,0:T(8,128)(2,1)S(1)}, bf16[8,256,1024]{2,1,0:T(8,128)(2,1)S(1)}) custom-call(bf16[128,2048]{1,0:T(8,128)(2,1)S(1)} %get-tuple-element.712.refs_0_, bf16[128,2048]{1,0:T(8,128)(2,1)S(1)} %get-tuple-element.722.refs_1_, ...), custom_call_target="tpu_custom_call" | custom-call | flops 2147483648 | bytes 8388608 | tf_op jit(solution)/shard_map/pallas_call | solution.py:352
  147.9 9.3 %shard_map.288 = (bf16[8,256,128]{2,1,0:T(8,128)(2,1)S(1)}, bf16[256,1024]{1,0:T(8,128)(2,1)S(1)}, bf16[8,256,1024]{2,1,0:T(8,128)(2,1)S(1)}) custom-call(bf16[128,2048]{1,0:T(8,128)(2,1)S(1)} %get-tuple-element.713.refs_0_, bf16[128,2048]{1,0:T(8,128)(2,1)S(1)} %get-tuple-element.723.refs_1_, ...), custom_call_target="tpu_custom_call" | custom-call | flops 2147483648 | bytes 8388608 | tf_op jit(solution)/shard_map/pallas_call | solution.py:352
  162.7 11.5 %collective-permute-done.27 = bf16[512,512]{1,0:T(8,128)(2,1)S(1)} collective-permute-done((bf16[512,512]{1,0:T(8,128)(2,1)S(1)}, bf16[512,512]{1,0:T(8,128)(2,1)S(1)}, u32[]{:S(2)}, u32[]{:S(2)}) %collective-permute-start.27) | collective-permute-done | bytes 524320 | tf_op jit(solution)/shard_map/ppermute | solution.py:66
  188.7 6.8 collective-permute-start.31
  197.0 18.1 %collective-permute-done.35 = bf16[256,2048]{1,0:T(8,128)(2,1)S(1)} collective-permute-done((bf16[256,2048]{1,0:T(8,128)(2,1)}, bf16[256,2048]{1,0:T(8,128)(2,1)S(1)}, u32[]{:S(2)}, u32[]{:S(2)}) %collective-permute-start.35) | collective-permute-done | bytes 1048608 | tf_op jit(solution)/shard_map/ppermute | solution.py:108
  216.4 9.4 %collective-permute-done.31 = bf16[128,2048]{1,0:T(8,128)(2,1)} collective-permute-done((bf16[128,2048]{1,0:T(8,128)(2,1)S(1)}, bf16[128,2048]{1,0:T(8,128)(2,1)}, u32[]{:S(2)}, u32[]{:S(2)}) %collective-permute-start.31) | collective-permute-done | bytes 524320 | tf_op jit(solution)/shard_map/ppermute | solution.py:71
  232.6 10.6 %collective-permute-done.39 = bf16[512,512]{1,0:T(8,128)(2,1)S(1)} collective-permute-done((bf16[512,512]{1,0:T(8,128)(2,1)S(1)}, bf16[512,512]{1,0:T(8,128)(2,1)S(1)}, u32[]{:S(2)}, u32[]{:S(2)}) %collective-permute-start.39) | collective-permute-done | bytes 524320 | tf_op jit(solution)/shard_map/ppermute | solution.py:66
  248.9 10.8 %shard_map.292 = (bf16[512,1024]{1,0:T(8,128)(2,1)S(1)}, bf16[512,1024]{1,0:T(8,128)(2,1)S(1)}, bf16[256,2048]{1,0:T(8,128)(2,1)S(1)}, bf16[256,2048]{1,0:T(8,128)(2,1)S(1)}, bf16[512,2048]{1,0:T(8,128)(2,1)S(1)}) custom-call(bf16[256,2048]{1,0:T(8,128)(2,1)S(1)} %constant_dynamic-update-slice_fusion.5.refs_0_, ...), custom_call_target="tpu_custom_call" | custom-call | flops 8589934592 | bytes 16777216 | tf_op jit(solution)/shard_map/pallas_call | solution.py:534
  269.6 10.8 %shard_map.293 = (bf16[512,1024]{1,0:T(8,128)(2,1)S(1)}, bf16[512,1024]{1,0:T(8,128)(2,1)S(1)}, bf16[256,2048]{1,0:T(8,128)(2,1)S(1)}, bf16[256,2048]{1,0:T(8,128)(2,1)S(1)}, bf16[512,2048]{1,0:T(8,128)(2,1)S(1)}) custom-call(bf16[256,2048]{1,0:T(8,128)(2,1)S(1)} %pad_maximum_fusion.11.refs_0_.refs_2_, ...), custom_call_target="tpu_custom_call" | custom-call | flops 8589934592 | bytes 16777216 | tf_op jit(solution)/shard_map/pallas_call | solution.py:534
  285.6 14.4 %collective-permute-done.49 = bf16[128,2048]{1,0:T(8,128)(2,1)S(1)} collective-permute-done((bf16[128,2048]{1,0:T(8,128)(2,1)S(1)}, bf16[128,2048]{1,0:T(8,128)(2,1)S(1)}, u32[]{:S(2)}, u32[]{:S(2)}) %collective-permute-start.49) | collective-permute-done | bytes 524320 | tf_op jit(solution)/shard_map/ppermute | solution.py:118
  305.3 11.9 %shard_map.294 = (bf16[512,1024]{1,0:T(8,128)(2,1)S(1)}, bf16[512,1024]{1,0:T(8,128)(2,1)S(1)}, bf16[256,2048]{1,0:T(8,128)(2,1)S(1)}, bf16[256,2048]{1,0:T(8,128)(2,1)S(1)}, bf16[512,2048]{1,0:T(8,128)(2,1)}) custom-call(bf16[256,2048]{1,0:T(8,128)(2,1)S(1)} %constant_dynamic-update-slice_fusion.7.refs_0_.refs_4_, ...), custom_call_target="tpu_custom_call" | custom-call | flops 8589934592 | bytes 16777216 | tf_op jit(solution)/shard_map/pallas_call | solution.py:534
  339.9 11.2 %shard_map.295 = (bf16[512,1024]{1,0:T(8,128)(2,1)S(1)}, bf16[512,1024]{1,0:T(8,128)(2,1)S(1)}, bf16[256,2048]{1,0:T(8,128)(2,1)S(1)}, bf16[256,2048]{1,0:T(8,128)(2,1)S(1)}, bf16[512,2048]{1,0:T(8,128)(2,1)S(1)}) custom-call(bf16[256,2048]{1,0:T(8,128)(2,1)S(1)} %copy-done.34, bf16[256,2048]{1,0:T(8,128)(2,1)} %collective-permute-done.58.refs_1_.refs_7_, ...), custom_call_target="tpu_custom_call" | custom-call | flops 8589934592 | bytes 16777216 | tf_op jit(solution)/shard_map/pallas_call | solution.py:534
  356.5 13.0 %shard_map.296 = bf16[4,512,1024]{2,1,0:T(8,128)(2,1)} custom-call(bf16[256,2048]{1,0:T(8,128)(2,1)S(1)} %copy-done.53, bf16[256,2048]{1,0:T(8,128)(2,1)S(1)} %copy-done.67, bf16[256,2048]{1,0:T(8,128)(2,1)S(1)} %copy-done.27, bf16[256,2048]{1,0:T(8,128)(2,1)S(1)} %copy-done.71, bf16[256,2048]{1,0:T(8,128)(2,1)S(1)} %copy-done.55, ...), custom_call_target="tpu_custom_call" | custom-call | flops 8589934592 | bytes 16777216 | tf_op jit(solution)/shard_map/pallas_call | solution.py:565
  407.0 13.8 %shard_map.297 = (bf16[256,1024]{1,0:T(8,128)(2,1)S(1)}, bf16[1024,256]{1,0:T(8,128)(2,1)S(1)}, f32[128,2048]{1,0:T(8,128)S(1)}, bf16[128,2048]{1,0:T(8,128)(2,1)S(1)}) custom-call(bf16[128,2048]{1,0:T(8,128)(2,1)S(1)} %get-tuple-element.530.refs_0_, bf16[128,2048]{1,0:T(8,128)(2,1)S(1)} %collective-permute-done.65.refs_1_, ...), custom_call_target="tpu_custom_call" | custom-call | flops 4294967296 | bytes 12582912 | tf_op jit(solution)/shard_map/pallas_call | solution.py:464
  428.7 13.5 %shard_map.298 = bf16[4,1024,512]{2,1,0:T(8,128)(2,1)} custom-call(bf16[512,1024]{1,0:T(8,128)(2,1)S(1)} %copy-done.83, bf16[512,1024]{1,0:T(8,128)(2,1)S(1)} %copy-done.85, bf16[512,1024]{1,0:T(8,128)(2,1)S(1)} %copy-done.87, bf16[512,1024]{1,0:T(8,128)(2,1)S(1)} %get-tuple-element.516.refs_3_, bf16[256,2048]{1,0:T(8,128)(2,1)} %pad_maximum_fusion.3.refs_2_.refs_4_, ...), custom_call_target="tpu_custom_call" | custom-call | flops 8589934592 | bytes 16777216 | tf_op jit(solution)/shard_map/pallas_call | solution.py:604
  477.6 13.9 %shard_map.299 = (bf16[256,1024]{1,0:T(8,128)(2,1)S(1)}, bf16[1024,256]{1,0:T(8,128)(2,1)S(1)}, f32[128,2048]{1,0:T(8,128)S(1)}, bf16[128,2048]{1,0:T(8,128)(2,1)S(1)}) custom-call(bf16[128,2048]{1,0:T(8,128)(2,1)S(1)} %get-tuple-element.537.refs_0_, bf16[128,2048]{1,0:T(8,128)(2,1)S(1)} %collective-permute-done.73.refs_1_, ...), custom_call_target="tpu_custom_call" | custom-call | flops 4294967296 | bytes 12582912 | tf_op jit(solution)/shard_map/pallas_call | solution.py:464
  515.6 7.8 %collective-permute-start.84 = (bf16[256,256]{1,0:T(8,128)(2,1)S(1)}, bf16[256,256]{1,0:T(8,128)(2,1)S(1)}, u32[]{:S(2)}, u32[]{:S(2)}) collective-permute-start(bf16[256,256]{1,0:T(8,128)(2,1)S(1)} %fusion.74), channel_id=1, source_target_pairs={{0,2},{1,3},{2,0},{3,1},{4,6},{5,7},{6,4},{7,5},{8,10},{9,11},{10,... | collective-permute-start | bytes 393224 | tf_op jit(solution)/shard_map/ppermute | solution.py:71
  523.4 12.0 %collective-permute-done.86 = bf16[1024,256]{1,0:T(8,128)(2,1)S(1)} collective-permute-done((bf16[1024,256]{1,0:T(8,128)(2,1)S(1)}, bf16[1024,256]{1,0:T(8,128)(2,1)S(1)}, u32[]{:S(2)}, u32[]{:S(2)}) %collective-permute-start.86) | collective-permute-done | bytes 524320 | tf_op jit(solution)/shard_map/ppermute | solution.py:66
  549.5 21.7 %collective-permute-done.93 = bf16[128,256]{1,0:T(8,128)(2,1)S(1)} collective-permute-done((bf16[128,256]{1,0:T(8,128)(2,1)S(1)}, bf16[128,256]{1,0:T(8,128)(2,1)S(1)}, u32[]{:S(2)}, u32[]{:S(2)}) %collective-permute-start.93) | collective-permute-done | bytes 65568 | tf_op jit(solution)/shard_map/ppermute | solution.py:66
  613.0 20.2 %collective-permute-start.104 = (f32[4,708]{1,0:T(4,128)S(1)}, f32[4,708]{1,0:T(4,128)S(1)}, u32[]{:S(2)}, u32[]{:S(2)}) collective-permute-start(f32[4,708]{1,0:T(4,128)S(1)} %select_bitcast_fusion), channel_id=1, source_target_pairs={{0,4},{1,5},{2,6},{3,7},{4,0},{5,1},{6,2},{7,3},{8,12},{9,13},{10,... | collective-permute-start | bytes 33992 | tf_op jit(solution)/shard_map/ppermute | solution.py:71
  671.7 7.7 %collective-permute-done.101 = bf16[128,2048]{1,0:T(8,128)(2,1)S(1)} collective-permute-done((bf16[128,2048]{1,0:T(8,128)(2,1)}, bf16[128,2048]{1,0:T(8,128)(2,1)S(1)}, u32[]{:S(2)}, u32[]{:S(2)}) %collective-permute-start.101) | collective-permute-done | bytes 524320 | tf_op jit(solution)/shard_map/ppermute | solution.py:71
  (898 shorter events, 386.5 us)
Async XLA Ops:
  7.2 69.3 %all-gather.2.cloned.1.call-start = ((), (), s32[]{:S(2)}) async-start(), calls=%async_computation | async-start | bytes 1351680 | tf_op jit(solution)/shard_map/all_gather | solution.py:660
  7.2 38.5 %collective-permute-start.4 = (bf16[512,1024]{1,0:T(8,128)(2,1)}, bf16[512,1024]{1,0:T(8,128)(2,1)S(1)}, u32[]{:S(2)}, u32[]{:S(2)}) collective-permute-start(bf16[512,1024]{1,0:T(8,128)(2,1)} %refs_4_.3), channel_id=1, source_target_pairs={{0,8},{8,0},{16,24},{24,16},{1,9},{9,1},{17,25},{25,17},{2,10},{10... | collective-permute-start | bytes 3145736 | tf_op jit(solution)/shard_map/ppermute | solution.py:66
  10.2 35.5 %collective-permute-start.5 = (bf16[512,1024]{1,0:T(8,128)(2,1)}, bf16[512,1024]{1,0:T(8,128)(2,1)S(1)}, u32[]{:S(2)}, u32[]{:S(2)}) collective-permute-start(bf16[512,1024]{1,0:T(8,128)(2,1)} %refs_4_.3), channel_id=1, source_target_pairs={{0,16},{8,24},{16,0},{24,8},{1,17},{9,25},{17,1},{25,9},{2,18},{10... | collective-permute-start | bytes 3145736 | tf_op jit(solution)/shard_map/ppermute | solution.py:66
  31.3 50.9 %collective-permute-start.15 = (bf16[128,2048]{1,0:T(8,128)(2,1)}, bf16[128,2048]{1,0:T(8,128)(2,1)}, u32[]{:S(2)}, u32[]{:S(2)}) collective-permute-start(bf16[128,2048]{1,0:T(8,128)(2,1)} %get-tuple-element.726), channel_id=1, source_target_pairs={{0,2},{1,3},{2,0},{3,1},{4,6},{5,7},{6,4},{7,5},{8,10},{9,11},{10,... | collective-permute-start | bytes 1572872 | tf_op jit(solution)/shard_map/ppermute | solution.py:71
  129.6 29.5 %collective-permute-start.25 = (bf16[256,2048]{1,0:T(8,128)(2,1)}, bf16[256,2048]{1,0:T(8,128)(2,1)S(1)}, u32[]{:S(2)}, u32[]{:S(2)}) collective-permute-start(bf16[256,2048]{1,0:T(8,128)(2,1)} %collective-permute-done.14), channel_id=1, source_target_pairs={{2,0},{3,1},{4,6},{5,7},{10,8},{11,9},{12,14},{13,15},{18,16},{19,... | collective-permute-start | bytes 3145736 | tf_op jit(solution)/shard_map/ppermute | solution.py:108
  131.8 28.6 %collective-permute-start.24 = (bf16[256,2048]{1,0:T(8,128)(2,1)}, bf16[256,2048]{1,0:T(8,128)(2,1)S(1)}, u32[]{:S(2)}, u32[]{:S(2)}) collective-permute-start(bf16[256,2048]{1,0:T(8,128)(2,1)} %pad_maximum_fusion.3.refs_2_.refs_4_), channel_id=1, source_target_pairs={{0,1},{1,0},{2,3},{3,2},{4,5},{5,4},{6,7},{7,6},{8,9},{9,8},{10,11... | collective-permute-start | bytes 3145736 | tf_op jit(solution)/shard_map/ppermute | solution.py:56
  182.8 32.3 %collective-permute-start.35 = (bf16[256,2048]{1,0:T(8,128)(2,1)}, bf16[256,2048]{1,0:T(8,128)(2,1)S(1)}, u32[]{:S(2)}, u32[]{:S(2)}) collective-permute-start(bf16[256,2048]{1,0:T(8,128)(2,1)} %copy-done.140), channel_id=1, source_target_pairs={{2,0},{3,1},{4,6},{5,7},{10,8},{11,9},{12,14},{13,15},{18,16},{19,... | collective-permute-start | bytes 3145736 | tf_op jit(solution)/shard_map/ppermute | solution.py:108
  184.1 32.3 %collective-permute-start.33 = (bf16[1024,512]{1,0:T(8,128)(2,1)}, bf16[1024,512]{1,0:T(8,128)(2,1)}, u32[]{:S(2)}, u32[]{:S(2)}) collective-permute-start(bf16[1024,512]{1,0:T(8,128)(2,1)} %refs_8_.3), channel_id=1, source_target_pairs={{0,8},{8,0},{16,24},{24,16},{1,9},{9,1},{17,25},{25,17},{2,10},{10... | collective-permute-start | bytes 3145736 | tf_op jit(solution)/shard_map/ppermute | solution.py:66
  184.5 31.9 %collective-permute-start.34 = (bf16[1024,512]{1,0:T(8,128)(2,1)}, bf16[1024,512]{1,0:T(8,128)(2,1)}, u32[]{:S(2)}, u32[]{:S(2)}) collective-permute-start(bf16[1024,512]{1,0:T(8,128)(2,1)} %refs_8_.3), channel_id=1, source_target_pairs={{0,16},{8,24},{16,0},{24,8},{1,17},{9,25},{17,1},{25,9},{2,18},{10... | collective-permute-start | bytes 3145736 | tf_op jit(solution)/shard_map/ppermute | solution.py:66
  188.7 37.1 %collective-permute-start.31 = (bf16[128,2048]{1,0:T(8,128)(2,1)S(1)}, bf16[128,2048]{1,0:T(8,128)(2,1)}, u32[]{:S(2)}, u32[]{:S(2)}) collective-permute-start(bf16[128,2048]{1,0:T(8,128)(2,1)S(1)} %get-tuple-element.380), channel_id=1, source_target_pairs={{0,2},{1,3},{2,0},{3,1},{4,6},{5,7},{6,4},{7,5},{8,10},{9,11},{10,... | collective-permute-start | bytes 1572872 | tf_op jit(solution)/shard_map/ppermute | solution.py:71
  195.5 30.3 %collective-permute-start.32 = (bf16[128,2048]{1,0:T(8,128)(2,1)S(1)}, bf16[128,2048]{1,0:T(8,128)(2,1)}, u32[]{:S(2)}, u32[]{:S(2)}) collective-permute-start(bf16[128,2048]{1,0:T(8,128)(2,1)S(1)} %get-tuple-element.380), channel_id=1, source_target_pairs={{2,4},{3,5},{4,2},{5,3},{10,12},{11,13},{12,10},{13,11},{18,20},{1... | collective-permute-start | bytes 1572872 | tf_op jit(solution)/shard_map/ppermute | solution.py:114
  321.5 29.7 %collective-permute-start.57 = (bf16[512,2048]{1,0:T(8,128)(2,1)}, bf16[512,2048]{1,0:T(8,128)(2,1)}, u32[]{:S(2)}, u32[]{:S(2)}) collective-permute-start(bf16[512,2048]{1,0:T(8,128)(2,1)} %get-tuple-element.447), channel_id=1, source_target_pairs={{0,1},{1,0},{2,3},{3,2},{4,5},{5,4},{6,7},{7,6},{8,9},{9,8},{10,11... | collective-permute-start | bytes 6291464 | tf_op jit(solution)/shard_map/ppermute | solution.py:56
  398.0 44.2 %collective-permute-start.71 = (bf16[512,1024]{1,0:T(8,128)(2,1)}, bf16[512,1024]{1,0:T(8,128)(2,1)S(1)}, u32[]{:S(2)}, u32[]{:S(2)}) collective-permute-start(bf16[512,1024]{1,0:T(8,128)(2,1)} %pad_maximum_fusion.13), channel_id=1, source_target_pairs={{0,8},{8,0},{16,24},{24,16},{1,9},{9,1},{17,25},{25,17},{2,10},{10... | collective-permute-start | bytes 3145736 | tf_op jit(solution)/shard_map/ppermute | solution.py:66
  399.7 42.5 %collective-permute-start.72 = (bf16[512,1024]{1,0:T(8,128)(2,1)}, bf16[512,1024]{1,0:T(8,128)(2,1)S(1)}, u32[]{:S(2)}, u32[]{:S(2)}) collective-permute-start(bf16[512,1024]{1,0:T(8,128)(2,1)} %pad_maximum_fusion.14), channel_id=1, source_target_pairs={{0,16},{8,24},{16,0},{24,8},{1,17},{9,25},{17,1},{25,9},{2,18},{10... | collective-permute-start | bytes 3145736 | tf_op jit(solution)/shard_map/ppermute | solution.py:66
  451.0 50.2 %collective-permute-start.80 = (bf16[256,2048]{1,0:T(8,128)(2,1)}, bf16[256,2048]{1,0:T(8,128)(2,1)}, u32[]{:S(2)}, u32[]{:S(2)}) collective-permute-start(bf16[256,2048]{1,0:T(8,128)(2,1)} %add_convert_fusion.10), channel_id=1, source_target_pairs={{0,2},{1,3},{6,4},{7,5},{8,10},{9,11},{14,12},{15,13},{16,18},{17,... | collective-permute-start | bytes 3145736 | tf_op jit(solution)/shard_map/ppermute | solution.py:122
  471.7 31.3 %collective-permute-start.81 = (bf16[256,2048]{1,0:T(8,128)(2,1)}, bf16[256,2048]{1,0:T(8,128)(2,1)}, u32[]{:S(2)}, u32[]{:S(2)}) collective-permute-start(bf16[256,2048]{1,0:T(8,128)(2,1)} %add_convert_fusion.6), channel_id=1, source_target_pairs={{0,2},{1,3},{6,4},{7,5},{8,10},{9,11},{14,12},{15,13},{16,18},{17,... | collective-permute-start | bytes 3145736 | tf_op jit(solution)/shard_map/ppermute | solution.py:122
  499.0 38.5 %collective-permute-start.87 = (bf16[1024,512]{1,0:T(8,128)(2,1)S(1)}, bf16[1024,512]{1,0:T(8,128)(2,1)S(1)}, u32[]{:S(2)}, u32[]{:S(2)}) collective-permute-start(bf16[1024,512]{1,0:T(8,128)(2,1)S(1)} %pad_maximum_fusion.17), channel_id=1, source_target_pairs={{0,8},{8,0},{16,24},{24,16},{1,9},{9,1},{17,25},{25,17},{2,10},{10... | collective-permute-start | bytes 3145736 | tf_op jit(solution)/shard_map/ppermute | solution.py:66
  501.2 36.3 %collective-permute-start.88 = (bf16[1024,512]{1,0:T(8,128)(2,1)S(1)}, bf16[1024,512]{1,0:T(8,128)(2,1)S(1)}, u32[]{:S(2)}, u32[]{:S(2)}) collective-permute-start(bf16[1024,512]{1,0:T(8,128)(2,1)S(1)} %pad_maximum_fusion.18), channel_id=1, source_target_pairs={{0,16},{8,24},{16,0},{24,8},{1,17},{9,25},{17,1},{25,9},{2,18},{10... | collective-permute-start | bytes 3145736 | tf_op jit(solution)/shard_map/ppermute | solution.py:66
  503.0 32.4 %collective-permute-start.86 = (bf16[1024,256]{1,0:T(8,128)(2,1)S(1)}, bf16[1024,256]{1,0:T(8,128)(2,1)S(1)}, u32[]{:S(2)}, u32[]{:S(2)}) collective-permute-start(bf16[1024,256]{1,0:T(8,128)(2,1)S(1)} %get-tuple-element.720), channel_id=1, source_target_pairs={{0,8},{8,0},{16,24},{24,16},{1,9},{9,1},{17,25},{25,17},{2,10},{10... | collective-permute-start | bytes 1572872 | tf_op jit(solution)/shard_map/ppermute | solution.py:66
  503.5 33.9 %collective-permute-start.85 = (bf16[1024,256]{1,0:T(8,128)(2,1)S(1)}, bf16[1024,256]{1,0:T(8,128)(2,1)S(1)}, u32[]{:S(2)}, u32[]{:S(2)}) collective-permute-start(bf16[1024,256]{1,0:T(8,128)(2,1)S(1)} %get-tuple-element.721), channel_id=1, source_target_pairs={{0,16},{8,24},{16,0},{24,8},{1,17},{9,25},{17,1},{25,9},{2,18},{10... | collective-permute-start | bytes 1572872 | tf_op jit(solution)/shard_map/ppermute | solution.py:66
  543.2 28.7 %collective-permute-start.94 = (bf16[256,2048]{1,0:T(8,128)(2,1)}, bf16[256,2048]{1,0:T(8,128)(2,1)S(1)}, u32[]{:S(2)}, u32[]{:S(2)}) collective-permute-start(bf16[256,2048]{1,0:T(8,128)(2,1)} %add_convert_fusion.4), channel_id=1, source_target_pairs={{2,4},{3,5},{4,2},{5,3},{10,12},{11,13},{12,10},{13,11},{18,20},{1... | collective-permute-start | bytes 3145736 | tf_op jit(solution)/shard_map/ppermute | solution.py:114
  543.9 29.6 %collective-permute-start.89 = (bf16[2048,256]{1,0:T(8,128)(2,1)}, bf16[2048,256]{1,0:T(8,128)(2,1)S(1)}, u32[]{:S(2)}, u32[]{:S(2)}) collective-permute-start(bf16[2048,256]{1,0:T(8,128)(2,1)} %pad_maximum_fusion.23), channel_id=1, source_target_pairs={{0,8},{8,0},{16,24},{24,16},{1,9},{9,1},{17,25},{25,17},{2,10},{10... | collective-permute-start | bytes 3145736 | tf_op jit(solution)/shard_map/ppermute | solution.py:66
  544.9 28.6 %collective-permute-start.90 = (bf16[2048,256]{1,0:T(8,128)(2,1)}, bf16[2048,256]{1,0:T(8,128)(2,1)S(1)}, u32[]{:S(2)}, u32[]{:S(2)}) collective-permute-start(bf16[2048,256]{1,0:T(8,128)(2,1)} %pad_maximum_fusion.24), channel_id=1, source_target_pairs={{0,16},{8,24},{16,0},{24,8},{1,17},{9,25},{17,1},{25,9},{2,18},{10... | collective-permute-start | bytes 3145736 | tf_op jit(solution)/shard_map/ppermute | solution.py:66
  585.1 48.1 %collective-permute-start.108 = (bf16[512,512]{1,0:T(8,128)(2,1)}, bf16[512,512]{1,0:T(8,128)(2,1)}, u32[]{:S(2)}, u32[]{:S(2)}) collective-permute-start(bf16[512,512]{1,0:T(8,128)(2,1)} %slice.795), channel_id=1, source_target_pairs={{0,2},{1,3},{6,4},{7,5},{8,10},{9,11},{14,12},{15,13},{16,18},{17,... | collective-permute-start | bytes 1572872 | tf_op jit(solution)/shard_map/ppermute | solution.py:122
  (262 other events, 3084.8 us)
Sparse Core Ops, SparseCore 0:
  21.5 54.9 all-gather.1

commit v3 on v1

--- a/solution.py
+++ b/solution.py
@@ -750,8 +750,13 @@
         out_first, context, cot_own, cot_far, cot_across
     )
     out_blocks = dp_second(out_first)
-    cot_far.append(line_out(cot_across[1]))
-    out_blocks, context, down_own, fixed = fence(out_blocks, context, down_weight, fixed)
+    half_size = cot_across[1].shape[0] // 2
+    cot_halves = [line_out(cot_across[1][:half_size])]
+    out_blocks, context, down_own, fixed, cot_halves, cot_across = fence(
+        out_blocks, context, down_weight, fixed, cot_halves, cot_across
+    )
+    cot_halves.append(line_out(cot_across[1][half_size:]))
+    cot_far.append(jnp.concatenate(cot_halves, axis=0))
     down_first = dp_first(down_own)
     middle, normed_two = [], []
     for m in range(micro):

time: 686 us -> 687 us (level)
  waiting for transfers between devices: 198 us -> 184 us
  local copies, waits for them, and re-layouts: 66 us -> 77.4 us
    ppermute x38, waiting for transfers between devices: 92.3 us -> 82.8 us  [swap_dp(): return lax.ppermute(block, 'dp', [(i, i ^ bit) for i in range(count)])]
    unnamed x358 -> x386, local copies, waits for them, and re-layouts: 20.9 us -> 25.4 us
    ppermute x5 -> x6, waiting for transfers between devices: 34.5 us -> 38.5 us  [line_out(): outward = lax.ppermute(across, 'mp', line_pairs([(1, 0), (2, 3)]))]
  transfers between devices with their start and end apart: 114 -> 115, of which waited for: 39 -> 38; matrix products, arithmetic and copies ran while one was open for 22% -> 24% of each run, Pallas kernels for 18% -> 17%
where the time goes in v3:
time: 687 us; the launch traced here: 677 us
  waiting for transfers between devices  184 us (27%)
  starting transfers between devices  153 us (22%)
  Pallas kernels  120 us (17%)
  other arithmetic  109 us (16%)
  local copies, waits for them, and re-layouts  77.4 us (11%)
  between operations  18.2 us (3%)
  matrix products  14.9 us (2%)
    ppermute x38, waiting for transfers between devices, swap_dp(): return lax.ppermute(block, 'dp', [(i, i ^ bit) for i in range(count)])  82.8 us
    pallas_call x4, Pallas kernels, mlp(): pl.pallas_call(lambda *refs: mlp_kernel(n, *refs), out_shape=[shaped((2 *...  44.1 us
    ppermute x17, starting transfers between devices, swap_mp(): return lax.ppermute(block, 'mp', [(i, i ^ bit) for i in range(count)])  41 us
    ppermute x38, starting transfers between devices, swap_dp(): return lax.ppermute(block, 'dp', [(i, i ^ bit) for i in range(count)])  40.2 us
    ppermute x6, waiting for transfers between devices, line_out(): outward = lax.ppermute(across, 'mp', line_pairs([(1, 0), (2, 3)]))  38.5 us
    convert_element_type x25, other arithmetic, plus(): return (left.astype(WIDE) + right.astype(WIDE)).astype(LOW)  36.6 us
    ppermute x9, starting transfers between devices, move_in(): return lax.ppermute(block, 'mp', line_pairs([(0, 1), (3, 2)]))  34.9 us
    pallas_call x2, Pallas kernels, attend_back(): pl.pallas_call(lambda *refs: attend_back_kernel(n, heads, (places, size),...  28 us
  transfers between devices with their start and end apart: 115, of which 38 were waited for; matrix products, arithmetic and copies ran while one was open for 24% of the time, Pallas kernels for 17%

profile of v3, /device:TPU:0, one launch (start us, length us, event | category | flops | bytes accessed | tf_op | source)
XLA Modules:
  0.0 676.9 jit_solution(11536541082027570307)
XLA Ops:
  39.3 8.0 %collective-permute-done.3 = bf16[128,2048]{1,0:T(8,128)(2,1)S(1)} collective-permute-done((bf16[128,2048]{1,0:T(8,128)(2,1)S(1)}, bf16[128,2048]{1,0:T(8,128)(2,1)S(1)}, u32[]{:S(2)}, u32[]{:S(2)}) %collective-permute-start.3) | collective-permute-done | bytes 524320 | tf_op jit(solution)/shard_map/ppermute | solution.py:71
  60.1 12.1 %collective-permute-done.6 = bf16[1024,256]{1,0:T(8,128)(2,1)S(1)} collective-permute-done((bf16[1024,256]{1,0:T(8,128)(2,1)S(1)}, bf16[1024,256]{1,0:T(8,128)(2,1)S(1)}, u32[]{:S(2)}, u32[]{:S(2)}) %collective-permute-start.6) | collective-permute-done | bytes 524320 | tf_op jit(solution)/shard_map/ppermute | solution.py:108
  99.4 6.9 %collective-permute-start.16 = (bf16[256,256]{1,0:T(8,128)(2,1)S(1)}, bf16[256,256]{1,0:T(8,128)(2,1)S(1)}, u32[]{:S(2)}, u32[]{:S(2)}) collective-permute-start(bf16[256,256]{1,0:T(8,128)(2,1)S(1)} %fusion.16), channel_id=1, source_target_pairs={{0,2},{1,3},{2,0},{3,1},{4,6},{5,7},{6,4},{7,5},{8,10},{9,11},{10,... | collective-permute-start | bytes 393224 | tf_op jit(solution)/shard_map/ppermute | solution.py:71
  113.2 8.3 %collective-permute-done.19 = bf16[1024,256]{1,0:T(8,128)(2,1)} collective-permute-done((bf16[1024,256]{1,0:T(8,128)(2,1)}, bf16[1024,256]{1,0:T(8,128)(2,1)}, u32[]{:S(2)}, u32[]{:S(2)}) %collective-permute-start.19) | collective-permute-done | bytes 524320 | tf_op jit(solution)/shard_map/ppermute | solution.py:66
  145.7 9.2 %shard_map.289 = (bf16[8,256,128]{2,1,0:T(8,128)(2,1)S(1)}, bf16[256,1024]{1,0:T(8,128)(2,1)S(1)}, bf16[8,256,1024]{2,1,0:T(8,128)(2,1)S(1)}) custom-call(bf16[128,2048]{1,0:T(8,128)(2,1)S(1)} %get-tuple-element.700.refs_0_, bf16[128,2048]{1,0:T(8,128)(2,1)S(1)} %get-tuple-element.710.refs_1_, ...), custom_call_target="tpu_custom_call" | custom-call | flops 2147483648 | bytes 8388608 | tf_op jit(solution)/shard_map/pallas_call | solution.py:352
  157.0 9.3 %shard_map.288 = (bf16[8,256,128]{2,1,0:T(8,128)(2,1)S(1)}, bf16[256,1024]{1,0:T(8,128)(2,1)S(1)}, bf16[8,256,1024]{2,1,0:T(8,128)(2,1)S(1)}) custom-call(bf16[128,2048]{1,0:T(8,128)(2,1)S(1)} %get-tuple-element.701.refs_0_, bf16[128,2048]{1,0:T(8,128)(2,1)S(1)} %get-tuple-element.711.refs_1_, ...), custom_call_target="tpu_custom_call" | custom-call | flops 2147483648 | bytes 8388608 | tf_op jit(solution)/shard_map/pallas_call | solution.py:352
  172.6 14.6 %collective-permute-done.29 = bf16[128,2048]{1,0:T(8,128)(2,1)S(1)} collective-permute-done((bf16[128,2048]{1,0:T(8,128)(2,1)S(1)}, bf16[128,2048]{1,0:T(8,128)(2,1)S(1)}, u32[]{:S(2)}, u32[]{:S(2)}) %collective-permute-start.29) | collective-permute-done | bytes 524320 | tf_op jit(solution)/shard_map/ppermute | solution.py:108
  237.1 8.6 %collective-permute-done.40 = bf16[512,512]{1,0:T(8,128)(2,1)S(1)} collective-permute-done((bf16[512,512]{1,0:T(8,128)(2,1)S(1)}, bf16[512,512]{1,0:T(8,128)(2,1)S(1)}, u32[]{:S(2)}, u32[]{:S(2)}) %collective-permute-start.40) | collective-permute-done | bytes 524320 | tf_op jit(solution)/shard_map/ppermute | solution.py:66
  252.9 10.5 %shard_map.292 = (bf16[512,1024]{1,0:T(8,128)(2,1)S(1)}, bf16[512,1024]{1,0:T(8,128)(2,1)S(1)}, bf16[256,2048]{1,0:T(8,128)(2,1)S(1)}, bf16[256,2048]{1,0:T(8,128)(2,1)S(1)}, bf16[512,2048]{1,0:T(8,128)(2,1)S(1)}) custom-call(bf16[256,2048]{1,0:T(8,128)(2,1)S(1)} %constant_dynamic-update-slice_fusion.5.refs_0_, ...), custom_call_target="tpu_custom_call" | custom-call | flops 8589934592 | bytes 16777216 | tf_op jit(solution)/shard_map/pallas_call | solution.py:534
  271.5 10.9 %shard_map.293 = (bf16[512,1024]{1,0:T(8,128)(2,1)S(1)}, bf16[512,1024]{1,0:T(8,128)(2,1)S(1)}, bf16[256,2048]{1,0:T(8,128)(2,1)S(1)}, bf16[256,2048]{1,0:T(8,128)(2,1)S(1)}, bf16[512,2048]{1,0:T(8,128)(2,1)S(1)}) custom-call(bf16[256,2048]{1,0:T(8,128)(2,1)S(1)} %pad_maximum_fusion.12.refs_0_.refs_2_, ...), custom_call_target="tpu_custom_call" | custom-call | flops 8589934592 | bytes 16777216 | tf_op jit(solution)/shard_map/pallas_call | solution.py:534
  288.9 15.9 %collective-permute-done.50 = bf16[128,2048]{1,0:T(8,128)(2,1)S(1)} collective-permute-done((bf16[128,2048]{1,0:T(8,128)(2,1)}, bf16[128,2048]{1,0:T(8,128)(2,1)S(1)}, u32[]{:S(2)}, u32[]{:S(2)}) %collective-permute-start.50) | collective-permute-done | bytes 524320 | tf_op jit(solution)/shard_map/ppermute | solution.py:118
  309.8 11.7 %shard_map.294 = (bf16[512,1024]{1,0:T(8,128)(2,1)S(1)}, bf16[512,1024]{1,0:T(8,128)(2,1)S(1)}, bf16[256,2048]{1,0:T(8,128)(2,1)S(1)}, bf16[256,2048]{1,0:T(8,128)(2,1)S(1)}, bf16[512,2048]{1,0:T(8,128)(2,1)}) custom-call(bf16[256,2048]{1,0:T(8,128)(2,1)S(1)} %constant_dynamic-update-slice_fusion.7.refs_0_.refs_4_, ...), custom_call_target="tpu_custom_call" | custom-call | flops 8589934592 | bytes 16777216 | tf_op jit(solution)/shard_map/pallas_call | solution.py:534
  332.2 6.3 collective-permute-start.57
  346.1 10.9 %shard_map.295 = (bf16[512,1024]{1,0:T(8,128)(2,1)S(1)}, bf16[512,1024]{1,0:T(8,128)(2,1)S(1)}, bf16[256,2048]{1,0:T(8,128)(2,1)S(1)}, bf16[256,2048]{1,0:T(8,128)(2,1)S(1)}, bf16[512,2048]{1,0:T(8,128)(2,1)S(1)}) custom-call(bf16[256,2048]{1,0:T(8,128)(2,1)S(1)} %copy-done.42, bf16[256,2048]{1,0:T(8,128)(2,1)} %collective-permute-done.59.refs_1_.refs_7_, ...), custom_call_target="tpu_custom_call" | custom-call | flops 8589934592 | bytes 16777216 | tf_op jit(solution)/shard_map/pallas_call | solution.py:534
  361.5 13.0 %shard_map.296 = bf16[4,512,1024]{2,1,0:T(8,128)(2,1)} custom-call(bf16[256,2048]{1,0:T(8,128)(2,1)S(1)} %copy-done.63, bf16[256,2048]{1,0:T(8,128)(2,1)S(1)} %copy-done.77, bf16[256,2048]{1,0:T(8,128)(2,1)S(1)} %copy-done.35, bf16[256,2048]{1,0:T(8,128)(2,1)S(1)} %copy-done.81, bf16[256,2048]{1,0:T(8,128)(2,1)S(1)} %copy-done.65, ...), custom_call_target="tpu_custom_call" | custom-call | flops 8589934592 | bytes 16777216 | tf_op jit(solution)/shard_map/pallas_call | solution.py:565
  385.4 6.7 collective-permute-done.64
  409.1 13.9 %shard_map.297 = (bf16[256,1024]{1,0:T(8,128)(2,1)S(1)}, bf16[1024,256]{1,0:T(8,128)(2,1)S(1)}, f32[128,2048]{1,0:T(8,128)S(1)}, bf16[128,2048]{1,0:T(8,128)(2,1)S(1)}) custom-call(bf16[128,2048]{1,0:T(8,128)(2,1)S(1)} %get-tuple-element.525.refs_0_, bf16[128,2048]{1,0:T(8,128)(2,1)S(1)} %collective-permute-done.66.refs_1_, ...), custom_call_target="tpu_custom_call" | custom-call | flops 4294967296 | bytes 12582912 | tf_op jit(solution)/shard_map/pallas_call | solution.py:464
  429.8 12.8 %shard_map.298 = bf16[4,1024,512]{2,1,0:T(8,128)(2,1)} custom-call(bf16[512,1024]{1,0:T(8,128)(2,1)S(1)} %copy-done.93, bf16[512,1024]{1,0:T(8,128)(2,1)S(1)} %copy-done.95, bf16[512,1024]{1,0:T(8,128)(2,1)S(1)} %copy-done.97, bf16[512,1024]{1,0:T(8,128)(2,1)S(1)} %get-tuple-element.511.refs_3_, bf16[256,2048]{1,0:T(8,128)(2,1)S(1)} %copy-done.20, ...), custom_call_target="tpu_custom_call" | custom-call | flops 8589934592 | bytes 16777216 | tf_op jit(solution)/shard_map/pallas_call | solution.py:604
  480.9 14.1 %shard_map.299 = (bf16[256,1024]{1,0:T(8,128)(2,1)S(1)}, bf16[1024,256]{1,0:T(8,128)(2,1)S(1)}, f32[128,2048]{1,0:T(8,128)S(1)}, bf16[128,2048]{1,0:T(8,128)(2,1)S(1)}) custom-call(bf16[128,2048]{1,0:T(8,128)(2,1)S(1)} %get-tuple-element.532.refs_0_, bf16[128,2048]{1,0:T(8,128)(2,1)} %collective-permute-done.74.refs_1_, ...), custom_call_target="tpu_custom_call" | custom-call | flops 4294967296 | bytes 12582912 | tf_op jit(solution)/shard_map/pallas_call | solution.py:464
  517.6 7.1 %collective-permute-start.85 = (bf16[256,256]{1,0:T(8,128)(2,1)S(1)}, bf16[256,256]{1,0:T(8,128)(2,1)S(1)}, u32[]{:S(2)}, u32[]{:S(2)}) collective-permute-start(bf16[256,256]{1,0:T(8,128)(2,1)S(1)} %fusion.74), channel_id=1, source_target_pairs={{0,2},{1,3},{2,0},{3,1},{4,6},{5,7},{6,4},{7,5},{8,10},{9,11},{10,... | collective-permute-start | bytes 393224 | tf_op jit(solution)/shard_map/ppermute | solution.py:71
  524.7 14.0 %collective-permute-done.87 = bf16[1024,256]{1,0:T(8,128)(2,1)S(1)} collective-permute-done((bf16[1024,256]{1,0:T(8,128)(2,1)S(1)}, bf16[1024,256]{1,0:T(8,128)(2,1)S(1)}, u32[]{:S(2)}, u32[]{:S(2)}) %collective-permute-start.87) | collective-permute-done | bytes 524320 | tf_op jit(solution)/shard_map/ppermute | solution.py:66
  552.2 21.7 %collective-permute-done.94 = bf16[128,256]{1,0:T(8,128)(2,1)S(1)} collective-permute-done((bf16[128,256]{1,0:T(8,128)(2,1)S(1)}, bf16[128,256]{1,0:T(8,128)(2,1)S(1)}, u32[]{:S(2)}, u32[]{:S(2)}) %collective-permute-start.94) | collective-permute-done | bytes 65568 | tf_op jit(solution)/shard_map/ppermute | solution.py:66
  603.2 7.2 %collective-permute-start.99 = (bf16[1152,256]{1,0:T(8,128)(2,1)}, bf16[1152,256]{1,0:T(8,128)(2,1)S(1)}, u32[]{:S(2)}, u32[]{:S(2)}) collective-permute-start(bf16[1152,256]{1,0:T(8,128)(2,1)} %bitcast.84), channel_id=1, source_target_pairs={{0,2},{1,3},{6,4},{7,5},{8,10},{9,11},{14,12},{15,13},{16,18},{17,... | collective-permute-start | bytes 1769480 | tf_op jit(solution)/shard_map/ppermute | solution.py:122
  615.4 6.3 collective-permute-done.99
  (936 shorter events, 398.4 us)
Async XLA Ops:
  7.2 69.4 %all-gather.2.cloned.1.call-start = ((), (), s32[]{:S(2)}) async-start(), calls=%async_computation | async-start | bytes 1351680 | tf_op jit(solution)/shard_map/all_gather | solution.py:660
  7.2 40.3 %collective-permute-start.4 = (bf16[512,1024]{1,0:T(8,128)(2,1)}, bf16[512,1024]{1,0:T(8,128)(2,1)S(1)}, u32[]{:S(2)}, u32[]{:S(2)}) collective-permute-start(bf16[512,1024]{1,0:T(8,128)(2,1)} %refs_4_.3), channel_id=1, source_target_pairs={{0,8},{8,0},{16,24},{24,16},{1,9},{9,1},{17,25},{25,17},{2,10},{10... | collective-permute-start | bytes 3145736 | tf_op jit(solution)/shard_map/ppermute | solution.py:66
  10.2 37.3 %collective-permute-start.5 = (bf16[512,1024]{1,0:T(8,128)(2,1)}, bf16[512,1024]{1,0:T(8,128)(2,1)S(1)}, u32[]{:S(2)}, u32[]{:S(2)}) collective-permute-start(bf16[512,1024]{1,0:T(8,128)(2,1)} %refs_4_.3), channel_id=1, source_target_pairs={{0,16},{8,24},{16,0},{24,8},{1,17},{9,25},{17,1},{25,9},{2,18},{10... | collective-permute-start | bytes 3145736 | tf_op jit(solution)/shard_map/ppermute | solution.py:66
  34.2 53.8 %collective-permute-start.15 = (bf16[128,2048]{1,0:T(8,128)(2,1)}, bf16[128,2048]{1,0:T(8,128)(2,1)}, u32[]{:S(2)}, u32[]{:S(2)}) collective-permute-start(bf16[128,2048]{1,0:T(8,128)(2,1)} %get-tuple-element.714), channel_id=1, source_target_pairs={{0,2},{1,3},{2,0},{3,1},{4,6},{5,7},{6,4},{7,5},{8,10},{9,11},{10,... | collective-permute-start | bytes 1572872 | tf_op jit(solution)/shard_map/ppermute | solution.py:71
  138.7 29.5 %collective-permute-start.25 = (bf16[256,2048]{1,0:T(8,128)(2,1)}, bf16[256,2048]{1,0:T(8,128)(2,1)S(1)}, u32[]{:S(2)}, u32[]{:S(2)}) collective-permute-start(bf16[256,2048]{1,0:T(8,128)(2,1)} %collective-permute-done.14), channel_id=1, source_target_pairs={{2,0},{3,1},{4,6},{5,7},{10,8},{11,9},{12,14},{13,15},{18,16},{19,... | collective-permute-start | bytes 3145736 | tf_op jit(solution)/shard_map/ppermute | solution.py:108
  140.8 27.6 %collective-permute-start.24 = (bf16[256,2048]{1,0:T(8,128)(2,1)S(1)}, bf16[256,2048]{1,0:T(8,128)(2,1)S(1)}, u32[]{:S(2)}, u32[]{:S(2)}) collective-permute-start(bf16[256,2048]{1,0:T(8,128)(2,1)S(1)} %pad_maximum_fusion.3.refs_2_.refs_4_), channel_id=1, source_target_pairs={{0,1},{1,0},{2,3},{3,2},{4,5},{5,4},{6,7},{7,6},{8,9},{9,8},{10,11... | collective-permute-start | bytes 3145736 | tf_op jit(solution)/shard_map/ppermute | solution.py:56
  141.0 27.4 %collective-permute-start.26 = (bf16[256,2048]{1,0:T(8,128)(2,1)S(1)}, bf16[256,2048]{1,0:T(8,128)(2,1)S(1)}, u32[]{:S(2)}, u32[]{:S(2)}) collective-permute-start(bf16[256,2048]{1,0:T(8,128)(2,1)S(1)} %copy-done.22), channel_id=1, source_target_pairs={{2,4},{3,5},{4,2},{5,3},{10,12},{11,13},{12,10},{13,11},{18,20},{1... | collective-permute-start | bytes 3145736 | tf_op jit(solution)/shard_map/ppermute | solution.py:101
  142.2 26.2 %collective-permute-start.17 = (bf16[1024,512]{1,0:T(8,128)(2,1)S(1)}, bf16[1024,512]{1,0:T(8,128)(2,1)S(1)}, u32[]{:S(2)}, u32[]{:S(2)}) collective-permute-start(bf16[1024,512]{1,0:T(8,128)(2,1)S(1)} %pad_maximum_fusion.7.refs_1_.refs_2_), channel_id=1, source_target_pairs={{0,8},{8,0},{16,24},{24,16},{1,9},{9,1},{17,25},{25,17},{2,10},{10... | collective-permute-start | bytes 3145736 | tf_op jit(solution)/shard_map/ppermute | solution.py:66
  326.0 31.1 %collective-permute-start.58 = (bf16[512,2048]{1,0:T(8,128)(2,1)}, bf16[512,2048]{1,0:T(8,128)(2,1)}, u32[]{:S(2)}, u32[]{:S(2)}) collective-permute-start(bf16[512,2048]{1,0:T(8,128)(2,1)} %get-tuple-element.442), channel_id=1, source_target_pairs={{0,1},{1,0},{2,3},{3,2},{4,5},{5,4},{6,7},{7,6},{8,9},{9,8},{10,11... | collective-permute-start | bytes 6291464 | tf_op jit(solution)/shard_map/ppermute | solution.py:56
  331.4 25.7 %collective-permute-start.56 = (bf16[128,2048]{1,0:T(8,128)(2,1)S(1)}, bf16[128,2048]{1,0:T(8,128)(2,1)S(1)}, u32[]{:S(2)}, u32[]{:S(2)}) collective-permute-start(bf16[128,2048]{1,0:T(8,128)(2,1)S(1)} %add_convert_fusion.29), channel_id=1, source_target_pairs={{2,4},{3,5},{4,2},{5,3},{10,12},{11,13},{12,10},{13,11},{18,20},{1... | collective-permute-start | bytes 1572872 | tf_op jit(solution)/shard_map/ppermute | solution.py:114
  401.2 41.5 %collective-permute-start.72 = (bf16[512,1024]{1,0:T(8,128)(2,1)}, bf16[512,1024]{1,0:T(8,128)(2,1)}, u32[]{:S(2)}, u32[]{:S(2)}) collective-permute-start(bf16[512,1024]{1,0:T(8,128)(2,1)} %pad_maximum_fusion.14), channel_id=1, source_target_pairs={{0,8},{8,0},{16,24},{24,16},{1,9},{9,1},{17,25},{25,17},{2,10},{10... | collective-permute-start | bytes 3145736 | tf_op jit(solution)/shard_map/ppermute | solution.py:66
  401.6 41.1 %collective-permute-start.73 = (bf16[512,1024]{1,0:T(8,128)(2,1)}, bf16[512,1024]{1,0:T(8,128)(2,1)}, u32[]{:S(2)}, u32[]{:S(2)}) collective-permute-start(bf16[512,1024]{1,0:T(8,128)(2,1)} %pad_maximum_fusion.15), channel_id=1, source_target_pairs={{0,16},{8,24},{16,0},{24,8},{1,17},{9,25},{17,1},{25,9},{2,18},{10... | collective-permute-start | bytes 3145736 | tf_op jit(solution)/shard_map/ppermute | solution.py:66
  453.9 49.3 %collective-permute-start.81 = (bf16[256,2048]{1,0:T(8,128)(2,1)}, bf16[256,2048]{1,0:T(8,128)(2,1)}, u32[]{:S(2)}, u32[]{:S(2)}) collective-permute-start(bf16[256,2048]{1,0:T(8,128)(2,1)} %add_convert_fusion.10), channel_id=1, source_target_pairs={{0,2},{1,3},{6,4},{7,5},{8,10},{9,11},{14,12},{15,13},{16,18},{17,... | collective-permute-start | bytes 3145736 | tf_op jit(solution)/shard_map/ppermute | solution.py:122
  475.7 29.2 %collective-permute-start.82 = (bf16[256,2048]{1,0:T(8,128)(2,1)}, bf16[256,2048]{1,0:T(8,128)(2,1)}, u32[]{:S(2)}, u32[]{:S(2)}) collective-permute-start(bf16[256,2048]{1,0:T(8,128)(2,1)} %add_convert_fusion.6), channel_id=1, source_target_pairs={{0,2},{1,3},{6,4},{7,5},{8,10},{9,11},{14,12},{15,13},{16,18},{17,... | collective-permute-start | bytes 3145736 | tf_op jit(solution)/shard_map/ppermute | solution.py:122
  502.4 37.7 %collective-permute-start.88 = (bf16[1024,512]{1,0:T(8,128)(2,1)S(1)}, bf16[1024,512]{1,0:T(8,128)(2,1)S(1)}, u32[]{:S(2)}, u32[]{:S(2)}) collective-permute-start(bf16[1024,512]{1,0:T(8,128)(2,1)S(1)} %pad_maximum_fusion.18), channel_id=1, source_target_pairs={{0,8},{8,0},{16,24},{24,16},{1,9},{9,1},{17,25},{25,17},{2,10},{10... | collective-permute-start | bytes 3145736 | tf_op jit(solution)/shard_map/ppermute | solution.py:66
  503.3 36.9 %collective-permute-start.89 = (bf16[1024,512]{1,0:T(8,128)(2,1)S(1)}, bf16[1024,512]{1,0:T(8,128)(2,1)S(1)}, u32[]{:S(2)}, u32[]{:S(2)}) collective-permute-start(bf16[1024,512]{1,0:T(8,128)(2,1)S(1)} %pad_maximum_fusion.19), channel_id=1, source_target_pairs={{0,16},{8,24},{16,0},{24,8},{1,17},{9,25},{17,1},{25,9},{2,18},{10... | collective-permute-start | bytes 3145736 | tf_op jit(solution)/shard_map/ppermute | solution.py:66
  504.9 33.8 %collective-permute-start.87 = (bf16[1024,256]{1,0:T(8,128)(2,1)S(1)}, bf16[1024,256]{1,0:T(8,128)(2,1)S(1)}, u32[]{:S(2)}, u32[]{:S(2)}) collective-permute-start(bf16[1024,256]{1,0:T(8,128)(2,1)S(1)} %get-tuple-element.708), channel_id=1, source_target_pairs={{0,8},{8,0},{16,24},{24,16},{1,9},{9,1},{17,25},{25,17},{2,10},{10... | collective-permute-start | bytes 1572872 | tf_op jit(solution)/shard_map/ppermute | solution.py:66
  506.7 33.2 %collective-permute-start.86 = (bf16[1024,256]{1,0:T(8,128)(2,1)S(1)}, bf16[1024,256]{1,0:T(8,128)(2,1)S(1)}, u32[]{:S(2)}, u32[]{:S(2)}) collective-permute-start(bf16[1024,256]{1,0:T(8,128)(2,1)S(1)} %get-tuple-element.709), channel_id=1, source_target_pairs={{0,16},{8,24},{16,0},{24,8},{1,17},{9,25},{17,1},{25,9},{2,18},{10... | collective-permute-start | bytes 1572872 | tf_op jit(solution)/shard_map/ppermute | solution.py:66
  545.9 28.8 %collective-permute-start.95 = (bf16[256,2048]{1,0:T(8,128)(2,1)}, bf16[256,2048]{1,0:T(8,128)(2,1)S(1)}, u32[]{:S(2)}, u32[]{:S(2)}) collective-permute-start(bf16[256,2048]{1,0:T(8,128)(2,1)} %add_convert_fusion.4), channel_id=1, source_target_pairs={{2,4},{3,5},{4,2},{5,3},{10,12},{11,13},{12,10},{13,11},{18,20},{1... | collective-permute-start | bytes 3145736 | tf_op jit(solution)/shard_map/ppermute | solution.py:114
  546.6 29.6 %collective-permute-start.90 = (bf16[2048,256]{1,0:T(8,128)(2,1)}, bf16[2048,256]{1,0:T(8,128)(2,1)S(1)}, u32[]{:S(2)}, u32[]{:S(2)}) collective-permute-start(bf16[2048,256]{1,0:T(8,128)(2,1)} %pad_maximum_fusion.24), channel_id=1, source_target_pairs={{0,8},{8,0},{16,24},{24,16},{1,9},{9,1},{17,25},{25,17},{2,10},{10... | collective-permute-start | bytes 3145736 | tf_op jit(solution)/shard_map/ppermute | solution.py:66
  547.7 28.5 %collective-permute-start.91 = (bf16[2048,256]{1,0:T(8,128)(2,1)}, bf16[2048,256]{1,0:T(8,128)(2,1)S(1)}, u32[]{:S(2)}, u32[]{:S(2)}) collective-permute-start(bf16[2048,256]{1,0:T(8,128)(2,1)} %pad_maximum_fusion.25), channel_id=1, source_target_pairs={{0,16},{8,24},{16,0},{24,8},{1,17},{9,25},{17,1},{25,9},{2,18},{10... | collective-permute-start | bytes 3145736 | tf_op jit(solution)/shard_map/ppermute | solution.py:66
  586.7 48.4 %collective-permute-start.96 = (bf16[128,2048]{1,0:T(8,128)(2,1)}, bf16[128,2048]{1,0:T(8,128)(2,1)}, u32[]{:S(2)}, u32[]{:S(2)}) collective-permute-start(bf16[128,2048]{1,0:T(8,128)(2,1)} %get-tuple-element.576), channel_id=1, source_target_pairs={{0,2},{1,3},{2,0},{3,1},{4,6},{5,7},{6,4},{7,5},{8,10},{9,11},{10,... | collective-permute-start | bytes 1572872 | tf_op jit(solution)/shard_map/ppermute | solution.py:71
  587.9 40.5 %collective-permute-start.112 = (bf16[1024,512]{1,0:T(8,128)(2,1)}, bf16[1024,512]{1,0:T(8,128)(2,1)}, u32[]{:S(2)}, u32[]{:S(2)}) collective-permute-start(bf16[1024,512]{1,0:T(8,128)(2,1)} %pad_maximum_fusion.16), channel_id=1, source_target_pairs={{0,8},{8,0},{16,24},{24,16},{1,9},{9,1},{17,25},{25,17},{2,10},{10... | collective-permute-start | bytes 3145736 | tf_op jit(solution)/shard_map/ppermute | solution.py:66
  589.0 40.9 %collective-permute-start.113 = (bf16[1024,512]{1,0:T(8,128)(2,1)}, bf16[1024,512]{1,0:T(8,128)(2,1)}, u32[]{:S(2)}, u32[]{:S(2)}) collective-permute-start(bf16[1024,512]{1,0:T(8,128)(2,1)} %pad_maximum_fusion.17), channel_id=1, source_target_pairs={{0,16},{8,24},{16,0},{24,8},{1,17},{9,25},{17,1},{25,9},{2,18},{10... | collective-permute-start | bytes 3145736 | tf_op jit(solution)/shard_map/ppermute | solution.py:66
  (279 other events, 3378.2 us)
Sparse Core Ops, SparseCore 0:
  21.5 55.0 all-gather.1
